TPU v7x, 512 devices: a whole 4x8x8 slice. The times are simulated.
512 devices in a mesh: dp: 32 (over z, x), tp: 16 (over y, core).
Axes of the slice: x: 4, y: 8, z: 8, core: 2. Of those that a mesh axis runs over, the one named last changes fastest.
Arguments:
- queries: bfloat16 [3072, 128, 576], P('dp', 'tp'), may hold values from -12 to 12, as said below
- page_pool: bfloat16 [6144, 16, 576], P('dp'), may hold values from -6 to 6
- prefix_cache: bfloat16 [2, 384, 576], replicated, may hold values from -12 to 12
- page_table: int32 [3072, 2], P('dp'), may hold values from 0 to 191, as said below
- lengths: int32 [3072], P('dp'), may hold values from 1 to 32, as said below
- prefix_id: int32 [3072], P('dp'), may hold values from 0 to 1
- prefix_len: int32 [2], replicated, may hold values from 16 to 384, as said below
- move_list: int32 [32, 32, 3], P('dp'), may hold values from 0 to 95, as said below
- value_up: bfloat16 [128, 512, 128], P('tp'), may hold values from -0.25 to 0.25
- output_weight: bfloat16 [16384, 7168], P('tp', 'dp'), may hold values from -0.046875 to 0.046875
- residual: bfloat16 [3072, 7168], P('tp', 'dp'), may hold values from -4 to 4
Outputs:
- layer_out: bfloat16 [3072, 7168], P('tp', 'dp')
- new_pool: bfloat16 [6144, 16, 576], P('dp')
Inputs may be any that keep to these rules, and one draw needn't show every extreme that they name: The entries lie within the range; a few queries of some heads may be large. `page_table`: each rank's 96 rows hold each of its 192 local page numbers exactly once. `lengths`: every rank has a slot of exactly 32 own tokens. `prefix_len`: each is a multiple of 16; some prefix has exactly 384 tokens. `move_list`: each rank lists 32 distinct leaving slots. Moves 2m and 2m+1 of every rank r go to rank (r + o_m) mod 32, with 16 distinct offsets o_m in 1 to 31 that are the same for all ranks; so every rank sends exactly 2 requests to each of 16 ranks and nothing to the others. Move k into rank t takes the slot that t's own move k vacates, so every rank receives 32 requests.
All inputs are finite; a program needn't handle non-finite values.
Results may differ from a plain program's by a relative error of at most 0.0056.
Values may be sent and summed in bfloat16 or wider, within the bound.
A program may use at most 64 MiB of HBM per device.

v0:
```python
import jax
import jax.numpy as jnp
from jax import lax
from jax.sharding import PartitionSpec as P

KVL = 512
CAP = 2


softmax_scale = 192.0 ** (-0.5)
masked_score = -1e30


def partial_softmax(scores, usable):
    scores = jnp.where(usable, scores, masked_score)
    highest = jnp.max(scores, axis=2)
    raised = jnp.exp(scores - highest[:, :, None])
    totals = jnp.sum(raised, axis=2)
    weights = raised.astype(jnp.bfloat16)
    return (highest, totals, weights)


def local(
    queries,
    page_pool,
    prefix_cache,
    page_table,
    lengths,
    prefix_id,
    prefix_len,
    move_list,
    value_up,
    output_weight,
    residual,
):
    rank_count = lax.axis_size("dp")
    requests, per_request = page_table.shape
    pool_pages, page_size, latent = page_pool.shape
    move_rows = move_list[0]
    leaving_slot = move_rows[:, 0]
    target = move_rows[:, 1]
    target_slot = move_rows[:, 2]
    move_count = move_rows.shape[0]
    move_index = jnp.arange(move_count, dtype=jnp.int32)
    before = (move_index[None, :] < move_index[:, None]) & (target[None, :] == target[:, None])
    buffer_slot = jnp.sum(before.astype(jnp.int32), axis=1)
    request_width = per_request * page_size * latent
    leaving = page_pool[page_table[leaving_slot]].reshape(move_count, request_width)
    outgoing = (
        jnp.zeros((rank_count, CAP, request_width), page_pool.dtype)
        .at[target, buffer_slot]
        .set(leaving)
    )
    labels = jnp.full((rank_count, CAP), -1, jnp.int32).at[target, buffer_slot].set(target_slot)
    arrived, arrived_slot = (
        lax.all_to_all(outgoing, "dp", split_axis=0, concat_axis=0, tiled=True),
        lax.all_to_all(labels, "dp", split_axis=0, concat_axis=0, tiled=True),
    )
    slot_list = arrived_slot.reshape(-1)
    destination = jnp.where(
        slot_list[:, None] >= 0, page_table[jnp.maximum(slot_list, 0)], pool_pages
    )
    new_pool = page_pool.at[destination.reshape(-1)].set(
        arrived.reshape(-1, page_size, latent), mode="drop"
    )
    prefix_count, prefix_rows = prefix_cache.shape[:2]
    key_table = prefix_cache.reshape(prefix_count * prefix_rows, latent)
    key_index = jnp.arange(prefix_count * prefix_rows, dtype=jnp.int32)
    key_owner = key_index // prefix_rows
    key_offset = key_index % prefix_rows
    owner_limit = jnp.sum(
        jnp.where(
            key_owner[:, None] == jnp.arange(prefix_count, dtype=jnp.int32)[None, :],
            prefix_len[None, :],
            0,
        ),
        axis=1,
    )
    prefix_usable = (key_owner[None, :] == prefix_id[:, None]) & (key_offset < owner_limit)[None, :]
    prefix_scores = (
        jnp.einsum("rhc,kc->rhk", queries, key_table, preferred_element_type=jnp.float32)
        * softmax_scale
    )
    high_pre, total_pre, weight_pre = partial_softmax(prefix_scores, prefix_usable[:, None, :])
    blend_pre = jnp.einsum(
        "rhk,kc->rhc", weight_pre, key_table[:, :KVL], preferred_element_type=jnp.float32
    )
    own_keys = new_pool[page_table].reshape(requests, per_request * page_size, latent)
    own_usable = jnp.arange(per_request * page_size, dtype=jnp.int32)[None, :] < lengths[:, None]
    own_scores = (
        jnp.einsum("rhc,rkc->rhk", queries, own_keys, preferred_element_type=jnp.float32)
        * softmax_scale
    )
    high_own, total_own, weight_own = partial_softmax(own_scores, own_usable[:, None, :])
    blend_own = jnp.einsum(
        "rhk,rkc->rhc", weight_own, own_keys[:, :, :KVL], preferred_element_type=jnp.float32
    )
    ceiling = jnp.maximum(high_pre, high_own)
    factor_pre = jnp.exp(high_pre - ceiling)
    factor_own = jnp.exp(high_own - ceiling)
    merged = (
        (factor_pre[:, :, None] * blend_pre + factor_own[:, :, None] * blend_own)
        / (factor_pre * total_pre + factor_own * total_own)[:, :, None]
    ).astype(jnp.bfloat16)
    heads_out = (
        jnp.einsum("rhc,hcv->rhv", merged, value_up, preferred_element_type=jnp.float32)
        .astype(jnp.bfloat16)
        .reshape(requests, -1)
    )
    partial_rows = jnp.dot(
        lax.all_gather(heads_out, "dp", axis=0, tiled=True),
        output_weight,
        preferred_element_type=jnp.float32,
    )
    summed = lax.psum_scatter(partial_rows, "tp", scatter_dimension=0, tiled=True)
    layer_out = (residual.astype(jnp.float32) + summed).astype(jnp.bfloat16)
    return (layer_out, new_pool)


def solution(mesh):
    in_specs = (
        P("dp", "tp", None),
        P("dp", None, None),
        P(),
        P("dp", None),
        P("dp"),
        P("dp"),
        P(),
        P("dp", None, None),
        P("tp", None, None),
        P("tp", "dp"),
        P("tp", "dp"),
    )
    out_specs = (P("tp", "dp"), P("dp", None, None))
    return jax.shard_map(local, mesh=mesh, in_specs=in_specs, out_specs=out_specs, check_vma=False)
```

profile of v0, /device:TPU:1, one launch (start us, length us, event | category | flops | bytes accessed | tf_op | source)
XLA Modules:
  0.0 328.2 jit_solution(10753640427571421640)
XLA Ops:
  7.2 4.5 %copy.124 = bf16[192,16,576]{2,1,0:T(8,128)(2,1)} copy(bf16[192,16,576]{2,1,0:T(8,128)(2,1)} %param.12) | data formatting | bytes 7077888
  11.9 2.0 scatter_fusion
  13.9 0.7 copy.76
  14.6 13.8 %all-to-all-start = ((s32[32,1,2]{2,1,0:T(1,128)}), s32[32,1,2]{2,1,0:T(1,128)}, u32[]{:S(2)}, u32[]{:S(2)}) async-start(s32[32,1,2]{2,1,0:T(1,128)} %copy.76), calls=%async_computation | async-start | bytes 32768 | tf_op jit(solution)/shard_map/all_to_all | solution.py:57
  28.6 0.6 gather_fusion.1
  29.5 2.9 gather_fusion.2
  32.4 1.6 reshape.262
  34.0 2.6 broadcast_in_dim.93
  36.6 25.3 %scatter_fusion.1 = bf16[32,2,18432]{2,1,0:T(2,128)(2,1)} fusion(bf16[32,2,18432]{2,1,0:T(2,128)(2,1)} %broadcast_in_dim.93, s32[32]{0:T(128)S(1)} %get-tuple-element.8, bf16[32,18432]{1,0:T(8,128)(2,1)S(1)} %reshape.262), kind=kCustom, calls=%fused_computation.5 | custom fusion | bytes 3539200 | tf_op jit(solution)/shard_map/scatter | solution.py:52
  61.9 9.1 %all-to-all-start.1 = ((bf16[32,2,18432]{2,1,0:T(2,128)(2,1)}), bf16[32,2,18432]{2,1,0:T(2,128)(2,1)S(1)}, u32[]{:S(2)}, u32[]{:S(2)}) async-start(bf16[32,2,18432]{2,1,0:T(2,128)(2,1)} %scatter_fusion.1), calls=%async_computation.1 | async-start | bytes 4718592 | tf_op jit(solution)/shard_map/all_to_all | solution.py:56
  71.3 3.0 copy.75
  74.3 2.2 copy.92
  76.7 3.3 %reshape.280 = bf16[768,576,1]{0,1,2:T(8,128)(2,1)} reshape(bf16[2,384,576]{1,0,2:T(2,128)(2,1)} %copy.75) | data formatting | bytes 1769472 | tf_op jit(solution)/shard_map/reshape | solution.py:67
  80.3 4.7 %fusion.2 = (f32[96,8]{1,0:T(8,128)}, f32[96,8,768]{2,1,0:T(8,128)}) fusion(pred[96,768]{1,0:T(8,128)(4,1)S(1)} %compare_and_fusion, bf16[96,8,576]{2,1,0:T(8,128)(2,1)} %param.11, bf16[768,576,1]{0,1,2:T(8,128)(2,1)} %reshape.280), kind=kOutput, calls=%fused_computation.11 | convolution fusion | flops 681245952 | bytes 4205568 | tf_op jit(solution)/shard_map/rhc,kc->rhk/dot_general | solution.py:81
  85.1 0.9 copy.84
  85.9 4.1 %fusion.3 = (f32[96,8]{1,0:T(8,128)}, bf16[96,8,768]{2,1,0:T(8,128)(2,1)}) fusion(f32[96,8,768]{2,1,0:T(8,128)} %get-tuple-element.13, f32[96,8]{1,0:T(8,128)} %get-tuple-element.12, pred[96,768]{1,0:T(8,128)(4,1)S(1)} %compare_and_fusion), kind=kLoop, calls=%fused_computation.12 | loop fusion | flops 2948352 | bytes 3618816 | tf_op jit(solution)/shard_map/reduce_sum | solution.py:18
  90.1 0.9 copy.89
  91.0 0.8 compare_reduce_fusion
  91.9 0.8 maximum_reduce_fusion
  92.8 0.6 gather_fusion
  93.7 30.8 %all-to-all-done.1 = bf16[32,2,18432]{2,1,0:T(2,128)(2,1)S(1)} async-done(((bf16[32,2,18432]{2,1,0:T(2,128)(2,1)}), bf16[32,2,18432]{2,1,0:T(2,128)(2,1)S(1)}, u32[]{:S(2)}, u32[]{:S(2)}) %all-to-all-start.1) | async-done | bytes 2359328 | tf_op jit(solution)/shard_map/all_to_all | solution.py:56
  124.5 3.6 %reshape.270 = bf16[128,16,576]{2,1,0:T(8,128)(2,1)} reshape(bf16[32,2,18432]{2,1,0:T(2,128)(2,1)S(1)} %all-to-all-done.1) | data formatting | bytes 4718592 | tf_op jit(solution)/shard_map/reshape | solution.py:64
  128.0 17.8 %scatter_fusion.2 = bf16[192,16,576]{2,1,0:T(8,128)(2,1)} fusion(bf16[192,16,576]{2,1,0:T(8,128)(2,1)} %copy.124, s32[128]{0:T(128)S(1)} %fusion.39, bf16[128,16,576]{2,1,0:T(8,128)(2,1)} %reshape.270), kind=kCustom, calls=%fused_computation.6 | custom fusion | bytes 7078400 | tf_op jit(solution)/shard_map/scatter | solution.py:63
  145.8 5.4 %gather_fusion.3 = bf16[192,16,576]{2,1,0:T(8,128)(2,1)} fusion(bf16[192,16,576]{2,1,0:T(8,128)(2,1)} %scatter_fusion.2, s32[1024]{0:T(1024)S(1)} %pad_clamp_fusion), kind=kCustom, calls=%fused_computation.3 | custom fusion | bytes 7078656 | tf_op jit(solution)/shard_map/gather | solution.py:88
  151.2 3.7 %fusion.44 = (f32[96,8]{1,0:T(8,128)S(1)}, f32[96,8,32]{2,1,0:T(8,128)S(1)}) fusion(bf16[96,32,576]{2,1,0:T(8,128)(2,1)} %bitcast.49, bf16[96,8,576]{2,1,0:T(8,128)(2,1)S(1)} %copy-done.4, pred[96,32]{1,0:T(8,128)(4,1)S(1)} %iota_compare_fusion), kind=kOutput, calls=%fused_computation.82 | convolution fusion | flops 28384512 | bytes 4528128 | tf_op jit(solution)/shard_map/rhc,rkc->rhk/dot_general | solution.py:91
  154.9 0.6 fusion
  156.0 3.5 %fusion.16 = bf16[8,12,8,128]{3,2,1,0:T(8,128)(2,1)S(1)} fusion(bf16[8,512,128]{2,1,0:T(8,128)(2,1)S(1)} %copy-done, f32[96,8,512]{2,1,0:T(8,128)S(1)} %fusion, bf16[96,8,768]{2,1,0:T(8,128)(2,1)} %get-tuple-element.6, bf16[768,576]{1,0:T(8,128)(2,1)} %bitcast.51, f32[96,8]{0,1:T(8,128)S(1)} %get-tuple-element.2, f32[96,8]{0,1:T(8,128)S(1)} %get-tuple-element.4, ...), kind=kOutput, calls=%fused_computation.24 | convolution fusion | flops 706707456 | bytes 4793344 | tf_op jit(solution)/shard_map/rhc,hcv->rhv/dot_general | solution.py:106
  159.5 0.7 copy.118
  160.3 94.7 %all-gather.2.cloned.1.call-done = bf16[3072,1024]{1,0:T(8,128)(2,1)} async-done(((bf16[96,1024]{1,0:T(8,128)(2,1)}), bf16[3072,1024]{1,0:T(8,128)(2,1)}) %all-gather.2.cloned.1.call-update) | async-done | bytes 6291472 | tf_op jit(solution)/shard_map/all_gather | solution.py:111
  255.0 6.3 %fusion.45 = f32[3072,224]{1,0:T(8,128)} fusion(bf16[3072,1024]{1,0:T(8,128)(2,1)} %all-gather.2.cloned.1.call-done, bf16[1024,224]{0,1:T(8,128)(2,1)S(1)} %copy-done.11), kind=kOutput, calls=%fused_computation.83 | convolution fusion | flops 1409286144 | bytes 9502720 | tf_op jit(solution)/shard_map/dot_general | solution.py:110
  261.3 58.4 %reduce-scatter.2.cloned.1.call-done = f32[192,224]{1,0:T(8,128)} async-done(((f32[3072,224]{1,0:T(8,128)}), f32[192,224]{1,0:T(8,128)}) %reduce-scatter.2.cloned.1.call-update) | async-done | bytes 172048 | tf_op jit(solution)/shard_map/reduce_scatter | solution.py:115
  319.8 1.6 add_convert_fusion
  (60 shorter events, 2.4 us)
Async XLA Ops:
  7.2 148.8 %copy-start = (bf16[8,512,128]{2,1,0:T(8,128)(2,1)S(1)}, bf16[8,512,128]{2,1,0:T(8,128)(2,1)}, u32[]{:S(2)}) copy-start(bf16[8,512,128]{2,1,0:T(8,128)(2,1)} %param.19) | copy-start | bytes 3145732
  7.2 21.3 %copy-start.6 = (s32[96,2]{0,1:T(2,128)S(1)}, s32[96,2]{0,1:T(2,128)}, u32[]{:S(2)}) copy-start(s32[96,2]{0,1:T(2,128)} %param.14) | copy-start | bytes 2308
  7.2 4.5 %copy-start.7 = (s32[1,32,3]{1,0,2:T(1,128)S(1)}, s32[1,32,3]{1,0,2:T(1,128)}, u32[]{:S(2)}) copy-start(s32[1,32,3]{1,0,2:T(1,128)} %param.18) | copy-start | bytes 1156
  14.6 47.3 %all-to-all-start = ((s32[32,1,2]{2,1,0:T(1,128)}), s32[32,1,2]{2,1,0:T(1,128)}, u32[]{:S(2)}, u32[]{:S(2)}) async-start(s32[32,1,2]{2,1,0:T(1,128)} %copy.76), calls=%async_computation | async-start | bytes 32768 | tf_op jit(solution)/shard_map/all_to_all | solution.py:57
  28.6 0.9 copy-start.2
  61.9 62.6 %all-to-all-start.1 = ((bf16[32,2,18432]{2,1,0:T(2,128)(2,1)}), bf16[32,2,18432]{2,1,0:T(2,128)(2,1)S(1)}, u32[]{:S(2)}, u32[]{:S(2)}) async-start(bf16[32,2,18432]{2,1,0:T(2,128)(2,1)} %scatter_fusion.1), calls=%async_computation.1 | async-start | bytes 4718592 | tf_op jit(solution)/shard_map/all_to_all | solution.py:56
  71.0 9.1 %copy-start.9 = (s32[2]{0:T(128)S(1)}, s32[2]{0:T(128)}, u32[]{:S(2)}) copy-start(s32[2]{0:T(128)} %param.17) | copy-start | bytes 28
  71.0 9.2 %copy-start.8 = (s32[96]{0:T(128)S(1)}, s32[96]{0:T(128)}, u32[]{:S(2)}) copy-start(s32[96]{0:T(128)} %param.16) | copy-start | bytes 1156
  71.0 184.0 %all-gather.2.cloned.1.call-start = ((), (), s32[]{:S(2)}) async-start(), calls=%async_computation.3 | async-start | bytes 6488064 | tf_op jit(solution)/shard_map/all_gather | solution.py:111
  85.0 5.9 %copy-start.10 = (s32[96]{0:T(128)S(1)}, s32[96]{0:T(128)}, u32[]{:S(2)}) copy-start(s32[96]{0:T(128)} %param.15) | copy-start | bytes 1156
  85.1 7.8 %copy-start.3 = (s32[96,2]{1,0:T(8,128)S(1)}, s32[96,2]{1,0:T(8,128)}, u32[]{:S(2)}) copy-start(s32[96,2]{1,0:T(8,128)} %copy-done.2) | copy-start | bytes 2308
  145.8 5.4 %copy-start.4 = (bf16[96,8,576]{2,1,0:T(8,128)(2,1)S(1)}, bf16[96,8,576]{2,1,0:T(8,128)(2,1)}, u32[]{:S(2)}) copy-start(bf16[96,8,576]{2,1,0:T(8,128)(2,1)} %param.11) | copy-start | bytes 2654212
  151.2 3.7 %copy-start.1 = (bf16[192,16,576]{2,1,0:T(8,128)(2,1)S(1)}, bf16[192,16,576]{2,1,0:T(8,128)(2,1)}, u32[]{:S(2)}) copy-start(bf16[192,16,576]{2,1,0:T(8,128)(2,1)} %gather_fusion.3) | copy-start | bytes 10616836
  156.0 99.0 %copy-start.11 = (bf16[1024,224]{0,1:T(8,128)(2,1)S(1)}, bf16[1024,224]{0,1:T(8,128)(2,1)}, u32[]{:S(2)}) copy-start(bf16[1024,224]{0,1:T(8,128)(2,1)} %param.20) | copy-start | bytes 1376260
  160.2 159.6 %reduce-scatter.2.cloned.1.call-start = ((), (), s32[]{:S(2)}) async-start(), calls=%async_computation.4 | async-start | bytes 3342336 | tf_op jit(solution)/shard_map/reduce_scatter | solution.py:115
  261.3 58.5 %copy-start.5 = (bf16[192,224]{1,0:T(8,128)(2,1)S(1)}, bf16[192,224]{1,0:T(8,128)(2,1)}, u32[]{:S(2)}) copy-start(bf16[192,224]{1,0:T(8,128)(2,1)} %param.21) | copy-start | bytes 258052
Sparse Core Ops, SparseCore 0:
  160.3 94.6 all-gather.1
  261.5 58.2 reduce-scatter.1
where the time goes:
time: 330 us; the launch traced here: 328 us
  waiting for transfers between devices  184 us (56%)
  local copies, waits for them, and re-layouts  79.7 us (24%)
  starting transfers between devices  23.2 us (7%)
  matrix products  18.8 us (6%)
  between operations  14.3 us (4%)
  other arithmetic  8.2 us (2%)
    all_gather x1, waiting for transfers between devices, local(): lax.all_gather(heads_out, 'dp', axis=0, tiled=True)  94.7 us
    reduce_scatter x1, waiting for transfers between devices, local(): lax.psum_scatter(partial_rows, 'tp', scatter_dimension=0, tiled=True)  58.4 us
    all_to_all x1, waiting for transfers between devices, local(): lax.all_to_all(outgoing, 'dp', split_axis=0, concat_axis=0, tiled=True)  30.8 us
    scatter x1, local copies, waits for them, and re-layouts, local(): outgoing = jnp.zeros((rank_count, CAP, request_width), page_pool.dtype).a...  25.3 us
    scatter x1, local copies, waits for them, and re-layouts, local(): page_pool.at[destination.reshape(-1)]  17.8 us
    all_to_all x1, starting transfers between devices, local(): lax.all_to_all(labels, 'dp', split_axis=0, concat_axis=0, tiled=True)  13.8 us
    all_to_all x1, starting transfers between devices, local(): lax.all_to_all(outgoing, 'dp', split_axis=0, concat_axis=0, tiled=True)  9.14 us
    unnamed x28, local copies, waits for them, and re-layouts  7.66 us
  transfers between devices with their start and end apart: 4, of which 3 were waited for; matrix products, arithmetic and copies ran while one was open for 17% of the time, Pallas kernels for 0%

commit v1 on v0

v1 whole, which is shorter than its diff:
```python
import functools

import jax
import jax.numpy as jnp
from jax import lax
from jax.experimental import pallas as pl
from jax.experimental.pallas import tpu as pltpu
from jax.sharding import PartitionSpec as P

MESH = pl.DeviceIdType.MESH

LAT = 576
KVL = 512
HEADS = 8
VH = 128
PAGE = 16
REQ = 96
MOVES = 32
CH = 32
CHUNKS = REQ // CH
ROWS = CH * HEADS
POOL = 192
PLEN = 384
NZ, NX, NY = 8, 4, 8
COLS = 224
DEPTH = HEADS * VH
SCALE = 192.0 ** (-0.5)
MASKED = -1e30

NT = (((1,), (1,)), ((), ()))

W0 = 0
PD = W0 + 4
PY = PD + 8
PC = PY + 8
Z0 = PC + 9
CX = Z0 + 8 * CHUNKS
RS = CX + CHUNKS
FX = RS + 8 * CHUNKS
PM = FX + 2
SEMS = PM + 7


def div(a, n):
    return lax.div(a, jnp.int32(n))


def rem(a, n):
    return lax.rem(a, jnp.int32(n))


def fused(
    perm_s, page_s, prefix_s, length_s, limit_s, leave_s, arrive_s,
    q_h, pool_h, kt_h, vup_h, wt_h, order_h, res_h,
    out_ref, arr_o,
    q_v, pool_v, kt_v, vup_v, w_v, order_v, res_v, order_r,
    stage, arr, q_f, keys, rowinfo, blend, stats, merged,
    zb, sx, rx, own, ss, rr, red, fx, fr,
    lsem, ssem, rsem,
):
    d = lax.axis_index("dp")
    t = lax.axis_index("tp")
    z, x = div(d, NX), rem(d, NX)
    y, c = div(t, 2), rem(t, 2)
    kind, quarter = div(t, 4), rem(t, 4)

    def at_x(v):
        return (z * NX + rem(v + NX, NX), t)

    def at_z(v):
        return (rem(v + NZ, NZ) * NX + x, t)

    def at_y(v):
        return (d, rem(v + NY, NY) * 2 + c)

    def at_rank(v):
        return (rem(v + 32, 32), t)

    partner = (d, y * 2 + 1 - c)
    final_core = div(x, 2)
    diagonal = c == final_core

    sent = []

    def remote(src, dst, device, slot, recv_slot=None):
        return pltpu.make_async_remote_copy(
            src_ref=src, dst_ref=dst, send_sem=ssem.at[slot],
            recv_sem=rsem.at[slot if recv_slot is None else recv_slot],
            device_id=device, device_id_type=MESH,
        )

    def send(src, dst, device, slot):
        copy = remote(src, dst, device, slot)
        copy.start()
        sent.append(copy)

    def arrived(dst, slot):
        remote(dst, dst, partner, slot).wait_recv()

    loads = {}
    for n, (name, src, dst) in enumerate([
        ("pool", pool_h, pool_v), ("q", q_h, q_v), ("kt", kt_h, kt_v), ("vup", vup_h, vup_v),
        ("w", wt_h, w_v.at[x]), ("order", order_h, order_v), ("res", res_h, res_v),
    ]):
        loads[name] = pltpu.make_async_copy(src, dst, lsem.at[n])
        loads[name].start()

    barrier = pltpu.get_barrier_semaphore()

    def greet(device):
        pl.semaphore_signal(barrier, inc=1, device_id=device, device_id_type=MESH)

    for device in (at_x(x + 1), at_x(x - 1), at_z(z + 1), at_z(z - 1), at_y(y + 1), at_y(y - 1), partner):
        greet(device)
    expected = jnp.int32(7)
    for i in range(8):
        offset = kind + 4 * i
        if i == 0:
            @pl.when(offset != 0)
            def _():
                greet(at_rank(d - offset))
        else:
            greet(at_rank(d - offset))
    expected = expected + jnp.where(kind == 0, 7, 8)
    for e in range(2):
        source_x = 2 * c + e

        @pl.when(jnp.logical_not(diagonal & (source_x == x)))
        def _():
            greet((z * NX + source_x, y * 2 + final_core))
    expected = expected + jnp.where(diagonal, 1, 2)

    @pl.when(z != y)
    def _():
        greet(at_z(y))
    expected = expected + jnp.where(z == y, 7, 0)
    pl.semaphore_wait(barrier, expected)


    def weights():
        send(wt_h, w_v.at[x], at_x(x + 1), W0)
        send(wt_h, w_v.at[x], at_x(x - 1), W0 + 1)
        yield
        half = COLS // 2
        low, high = rem(x + NX - 1, NX), rem(x + 1, NX)
        arrived(w_v.at[low], W0)
        send(w_v.at[low, pl.ds(0, half)], w_v.at[low, pl.ds(0, half)], at_x(x + 1), W0 + 2)
        arrived(w_v.at[high], W0 + 1)
        send(w_v.at[high, pl.ds(half, half)], w_v.at[high, pl.ds(half, half)], at_x(x - 1), W0 + 3)
        yield
        far = rem(x + 2, NX)
        arrived(w_v.at[far, pl.ds(0, half)], W0 + 2)
        arrived(w_v.at[far, pl.ds(half, half)], W0 + 3)
        loads["w"].wait()
        yield

    def ring(block, first, second, me, n, device, base, after=None):
        send(block(me), block(me), device(me + 1), base)
        send(block(me), block(me), device(me - 1), base + 1)
        yield
        for s in (1, 2, 3):
            low, high = rem(me + n - s, n), rem(me + s, n)
            arrived(block(low), base + 2 * s - 2)
            part = block if s < 3 else first
            send(part(low), part(low), device(me + 1), base + 2 * s)
            arrived(block(high), base + 2 * s - 1)
            part = block if s < 3 else second
            send(part(high), part(high), device(me - 1), base + 2 * s + 1)
            if after is not None:
                after(block(low), 2 * s - 2)
                after(block(high), 2 * s - 1)
            yield
        far = rem(me + 4, n)
        arrived(first(far), base + 6)
        arrived(second(far), base + 7)
        if after is not None:
            after(first(far), 6)
            after(second(far), 7)
        yield

    def pages():
        loads["pool"].wait()
        for i in range(8):
            offset = kind + 4 * i
            stage[i] = pool_v[leave_s[offset * 4 + quarter]]

            def go():
                remote(stage.at[i], arr.at[t * 8 + i], at_rank(d + offset), PD + i).start()
            if i == 0:
                pl.when(offset != 0)(go)

                @pl.when(offset == 0)
                def _():
                    arr[t * 8] = jnp.zeros((PAGE, LAT), arr.dtype)
            else:
                go()
        yield
        for i in range(8):
            def come():
                copy = remote(stage.at[i], arr.at[t * 8 + i], partner, PD + i)
                copy.wait_send()
                copy.wait_recv()
            if i == 0:
                pl.when(kind != 0)(come)
            else:
                come()

        def block(o, core=c):
            return arr.at[pl.ds((o * 2 + core) * 8, 8)]

        def first(o, core=c):
            return arr.at[pl.ds((o * 2 + core) * 8, 4)]

        def second(o, core=c):
            return arr.at[pl.ds((o * 2 + core) * 8 + 4, 4)]

        def hand(part, slot):
            send(part, part, partner, PC + 1 + slot)

        send(block(y), block(y), partner, PC)
        yield from ring(block, first, second, y, NY, at_y, PY, hand)
        other = 1 - c
        arrived(block(y, other), PC)
        for s in (1, 2, 3):
            arrived(block(rem(y + NY - s, NY), other), PC + 2 * s - 1)
            arrived(block(rem(y + s, NY), other), PC + 2 * s)
        far = rem(y + 4, NY)
        arrived(first(far, other), PC + 7)
        arrived(second(far, other), PC + 8)
        copy = pltpu.make_async_copy(arr, arr_o, lsem.at[7])
        copy.start()
        loads["arr"] = copy
        yield

    def prefix_part(n):
        def place(j, _):
            slot = perm_s[n * CH + j]
            q_f[j] = q_v[slot].astype(jnp.float32)
            prefix = prefix_s[slot]
            rowinfo[0, j] = jnp.full((HEADS, 128), prefix, jnp.int32)
            rowinfo[1, j] = jnp.full((HEADS, 128), limit_s[prefix], jnp.int32)
            rowinfo[2, j] = jnp.full((HEADS, 128), length_s[slot], jnp.int32)
            return 0

        lax.fori_loop(0, CH, place, 0)
        q = q_f[...].reshape(ROWS, LAT).astype(jnp.bfloat16)
        which = rowinfo[0].reshape(ROWS, 128)[:, :1] == 0
        limit = rowinfo[1].reshape(ROWS, 128)[:, :1]
        scores = jnp.where(
            which,
            jnp.dot(q, kt_v[0], preferred_element_type=jnp.float32),
            jnp.dot(q, kt_v[1], preferred_element_type=jnp.float32),
        ) * SCALE
        column = lax.broadcasted_iota(jnp.int32, (ROWS, PLEN), 1)
        scores = jnp.where(column < limit, scores, MASKED)
        highest = jnp.max(scores, axis=1, keepdims=True)
        raised = jnp.exp(scores - highest)
        total = jnp.sum(raised, axis=1, keepdims=True)
        stats[0] = jnp.broadcast_to(highest, (ROWS, 128))
        stats[1] = jnp.broadcast_to(total, (ROWS, 128))
        blend[...] = lax.dot_general(
            jnp.where(which, raised, 0.0).astype(jnp.bfloat16), kt_v[0, :KVL, :], NT,
            preferred_element_type=jnp.float32,
        ) + lax.dot_general(
            jnp.where(which, 0.0, raised).astype(jnp.bfloat16), kt_v[1, :KVL, :], NT,
            preferred_element_type=jnp.float32,
        )

    def own_part(n):
        def place(j, _):
            at = pl.multiple_of(j * 2 * PAGE, 2 * PAGE)
            if n < CHUNKS - 1:
                slot = perm_s[n * CH + j]
                keys[pl.ds(at, PAGE), :] = pool_v[page_s[slot]]
                keys[pl.ds(at + PAGE, PAGE), :] = pool_v[page_s[REQ + slot]]
            else:
                keys[pl.ds(at, PAGE), :] = arr[arrive_s[2 * j]]
                keys[pl.ds(at + PAGE, PAGE), :] = arr[arrive_s[2 * j + 1]]
            return 0

        lax.fori_loop(0, CH, place, 0)
        group = 64
        row = lax.broadcasted_iota(jnp.int32, (group, 256), 0)
        column = lax.broadcasted_iota(jnp.int32, (group, 256), 1)
        same = lax.shift_right_logical(row, 3) == lax.shift_right_logical(column, 5)
        token = column & 31
        for g in range(ROWS // group):
            rows = pl.ds(g * group, group)
            q = q_f[pl.ds(g * 8, 8)].reshape(group, LAT).astype(jnp.bfloat16)
            k = keys[pl.ds(g * 256, 256), :]
            length = rowinfo[2, pl.ds(g * 8, 8)].reshape(group, 128)[:, :1]
            scores = lax.dot_general(q, k, NT, preferred_element_type=jnp.float32) * SCALE
            scores = jnp.where(same & (token < length), scores, MASKED)
            high_own = jnp.max(scores, axis=1, keepdims=True)
            raised = jnp.exp(scores - high_own)
            total_own = jnp.sum(raised, axis=1, keepdims=True)
            blend_own = jnp.dot(
                raised.astype(jnp.bfloat16), keys[pl.ds(g * 256, 256), :KVL], preferred_element_type=jnp.float32
            )
            high_pre = stats[0, rows, :][:, :1]
            total_pre = stats[1, rows, :][:, :1]
            ceiling = jnp.maximum(high_pre, high_own)
            f = jnp.exp(high_pre - ceiling)
            h = jnp.exp(high_own - ceiling)
            mixed = (f * blend[rows, :] + h * blend_own) / (f * total_pre + h * total_own)
            for l in range(KVL // 128):
                merged[l, rows, :] = mixed[:, l * 128:(l + 1) * 128]
        mine = pl.ds(pl.multiple_of(z * CH, CH), CH)
        for h in range(HEADS):
            a = jnp.concatenate(
                [merged[l, pl.ds(h, CH, stride=HEADS), :] for l in range(KVL // 128)], axis=1
            ).astype(jnp.bfloat16)
            zb[n, mine, h * VH:(h + 1) * VH] = jnp.dot(
                a, vup_v[h], preferred_element_type=jnp.float32
            ).astype(jnp.bfloat16)

    def heads(n):
        def block(o):
            return zb.at[n, pl.ds(pl.multiple_of(o * CH, CH), CH)]

        def first(o):
            return zb.at[n, pl.ds(pl.multiple_of(o * CH, CH), CH // 2)]

        def second(o):
            return zb.at[n, pl.ds(pl.multiple_of(o * CH + CH // 2, CH // 2), CH // 2)]

        yield from ring(block, first, second, z, NZ, at_z, Z0 + 8 * n)

    def product(n):
        for i in range(2):
            sx[n, i] = lax.dot_general(
                zb[n], w_v[2 * (1 - c) + i], NT, preferred_element_type=jnp.float32
            ).astype(jnp.bfloat16)
        send(sx.at[n], rx.at[n], partner, CX + n)
        for i in range(2):
            own[n, i] = lax.dot_general(zb[n], w_v[2 * c + i], NT, preferred_element_type=jnp.float32)

    def sums(n):
        base = RS + 8 * n
        arrived(rx.at[n], CX + n)
        for i in range(2):
            own[n, i] = own[n, i] + rx[n, i].astype(jnp.float32)

        def mine(i, o):
            return own[n, i, pl.ds(pl.multiple_of(rem(o + 2 * NY, NY) * CH, CH), CH), :]

        up, down = at_y(y + 1), at_y(y - 1)
        ss[n, 0, 0, 0] = mine(0, y + 4).astype(jnp.bfloat16)
        send(ss.at[n, 0, 0, 0], rr.at[n, 0, 0, 0], up, base)
        ss[n, 1, 0, 1] = mine(1, y - 4).astype(jnp.bfloat16)
        send(ss.at[n, 1, 0, 1], rr.at[n, 1, 0, 1], down, base + 1)
        yield
        arrived(rr.at[n, 0, 0, 0], base)
        ss[n, 0, 1, 0] = (mine(0, y + 3) + rr[n, 0, 0, 0].astype(jnp.float32)).astype(jnp.bfloat16)
        ss[n, 0, 1, 1] = mine(1, y + 3).astype(jnp.bfloat16)
        send(ss.at[n, 0, 1], rr.at[n, 0, 1], up, base + 2)
        arrived(rr.at[n, 1, 0, 1], base + 1)
        ss[n, 1, 1, 1] = (mine(1, y - 3) + rr[n, 1, 0, 1].astype(jnp.float32)).astype(jnp.bfloat16)
        ss[n, 1, 1, 0] = mine(0, y - 3).astype(jnp.bfloat16)
        send(ss.at[n, 1, 1], rr.at[n, 1, 1], down, base + 3)
        yield
        for s in (2, 3):
            for way, device, o in ((0, up, y + 4 - s), (1, down, y - 4 + s)):
                arrived(rr.at[n, way, s - 1], base + 2 * (s - 1) + way)
                for i in range(2):
                    ss[n, way, s, i] = (mine(i, o) + rr[n, way, s - 1, i].astype(jnp.float32)).astype(jnp.bfloat16)
                send(ss.at[n, way, s], rr.at[n, way, s], device, base + 2 * s + way)
            yield
        arrived(rr.at[n, 0, 3], base + 6)
        arrived(rr.at[n, 1, 3], base + 7)
        for i in range(2):
            red[i, n * CH:(n + 1) * CH] = (
                mine(i, y) + rr[n, 0, 3, i].astype(jnp.float32) + rr[n, 1, 3, i].astype(jnp.float32)
            ).astype(jnp.bfloat16)
        yield

    def order_send():
        loads["order"].wait()

        @pl.when(z == y)
        def _():
            for s in range(1, NZ):
                remote(order_v, order_r, at_z(z + s), PM + s - 1, PM).start()

    def order_wait():
        @pl.when(z == y)
        def _():
            for s in range(1, NZ):
                remote(order_v, order_r, at_z(z + s), PM + s - 1, PM).wait_send()
            order_r[...] = order_v[...]

        @pl.when(z != y)
        def _():
            remote(order_v, order_r, at_z(y), PM, PM).wait_recv()

    def finish():
        order_wait()
        place = order_r[...][:, :REQ]
        slot = rem(x, 2)
        for i in range(2):
            fx[i] = jnp.dot(place, red[i], preferred_element_type=jnp.float32).astype(jnp.bfloat16)
            same = diagonal & (2 * c + i == x)
            copy = remote(fx.at[i], fr.at[slot], (z * NX + 2 * c + i, y * 2 + final_core), FX + i, FX + slot)

            @pl.when(same)
            def _():
                fr[slot] = fx[i]

            pl.when(jnp.logical_not(same))(copy.start)
        loads["res"].wait()
        for e in range(2):
            same = diagonal & (2 * c + e == x)
            copy = remote(fx.at[e], fr.at[e], partner, FX + e)
            pl.when(jnp.logical_not(same))(copy.wait_recv)
            rows = pl.ds(e * REQ, REQ)
            out_ref[rows, :] = (
                res_v[rows, :].astype(jnp.float32) + fr[e].astype(jnp.float32)
            ).astype(jnp.bfloat16)
        for i in range(2):
            same = diagonal & (2 * c + i == x)
            copy = remote(fx.at[i], fr.at[slot], partner, FX + i)
            pl.when(jnp.logical_not(same))(copy.wait_send)

    w = weights()
    p = pages()
    hs = [heads(n) for n in range(CHUNKS)]
    rs = [sums(n) for n in range(CHUNKS)]

    next(w)
    next(p)
    order_send()
    loads["q"].wait()
    loads["kt"].wait()
    prefix_part(0)
    loads["vup"].wait()
    own_part(0)
    next(hs[0])
    next(p)
    prefix_part(1)
    own_part(1)
    next(hs[1])
    next(p)
    next(w)
    next(hs[0])
    prefix_part(2)
    next(p)
    next(hs[0])
    next(hs[1])
    next(p)
    next(hs[0])
    next(hs[1])
    next(w)
    next(p)
    next(p)
    own_part(2)
    next(hs[2])
    next(hs[0])
    next(hs[1])
    product(0)
    next(hs[2])
    next(hs[1])
    next(rs[0])
    product(1)
    next(hs[2])
    next(rs[0])
    next(rs[1])
    next(hs[2])
    next(rs[0])
    next(rs[1])
    next(hs[2])
    product(2)
    next(rs[0])
    next(rs[1])
    next(rs[2])
    next(rs[0])
    next(rs[1])
    next(rs[2])
    next(rs[1])
    next(rs[2])
    next(rs[2])
    next(rs[2])
    finish()
    for copy in sent:
        copy.wait_send()
    loads["arr"].wait()


def place_pages(page_s, move_s, pool_h, arr_h, new_h, pool_v, sem):
    rank = lax.axis_index("dp")
    load = pltpu.make_async_copy(pool_h, pool_v, sem.at[0])
    load.start()
    load.wait()

    def come(k, _):
        slot = move_s[k]
        offset = rem(move_s[MOVES + k] - rank + 32, 32)
        source = (rem(offset, 4) * 4 + 2 * rem(k, 2)) * 8 + div(offset, 4)
        for p in range(2):
            pltpu.make_async_copy(arr_h.at[source + 8 * p], pool_v.at[page_s[p * REQ + slot]], sem.at[1]).start()
        return 0

    lax.fori_loop(0, MOVES, come, 0)
    pltpu.make_async_copy(arr_h.at[pl.ds(0, 2 * MOVES)], pool_v.at[pl.ds(0, 2 * MOVES)], sem.at[1]).wait()
    store = pltpu.make_async_copy(pool_v, new_h, sem.at[2])
    store.start()
    store.wait()


def local(
    queries, page_pool, prefix_cache, page_table, lengths, prefix_id, prefix_len,
    move_list, value_up, output_weight, residual,
):
    rank = lax.axis_index("dp")
    leaving = move_list[0, :, 0]
    offset = (move_list[0, :, 1] - rank + 32) % 32
    slots = jnp.arange(REQ, dtype=jnp.int32)
    moves = jnp.arange(MOVES, dtype=jnp.int32)
    is_left = leaving[None, :] == slots[:, None]
    left = jnp.any(is_left, axis=1)
    move_of = jnp.sum(jnp.where(is_left, moves[None, :], 0), axis=1)
    ahead = jnp.sum(jnp.where((slots[None, :] < slots[:, None]) & ~left[None, :], 1, 0), axis=1)
    position = jnp.where(left, REQ - MOVES + move_of, ahead)
    perm = jnp.sum(jnp.where(position[None, :] == slots[:, None], slots[None, :], 0), axis=1)
    order = (position[:, None] == jnp.arange(128, dtype=jnp.int32)[None, :]).astype(jnp.bfloat16)
    pages = page_table.T
    left_pages = jnp.sum(jnp.where(is_left[None, :, :], pages[:, :, None], 0), axis=1)
    by_pair = left_pages.reshape(2, 16, 2)
    hit = offset[::2][None, :] == jnp.arange(32, dtype=jnp.int32)[:, None]
    leave = jnp.sum(jnp.where(hit[:, :, None, None], by_pair.transpose(1, 2, 0)[None], 0), axis=1)
    arrive = ((offset % 4) * 4 + 2 * (moves % 2))[:, None] + jnp.arange(2, dtype=jnp.int32)[None, :]
    arrive = arrive * 8 + (offset // 4)[:, None]
    pages = pages.reshape(-1)
    arrive = arrive.reshape(-1)

    smem = pl.BlockSpec(memory_space=pltpu.SMEM)
    hbm = pl.BlockSpec(memory_space=pl.ANY)
    bf, f32 = jnp.bfloat16, jnp.float32
    vm = pltpu.VMEM
    layer_out, arr = pl.pallas_call(
        fused,
        out_shape=(
            jax.ShapeDtypeStruct((2 * REQ, COLS), bf),
            jax.ShapeDtypeStruct((128, PAGE, LAT), bf),
        ),
        in_specs=[smem] * 7 + [hbm] * 7,
        out_specs=(pl.BlockSpec(memory_space=pltpu.VMEM), hbm),
        scratch_shapes=[
            vm((REQ, HEADS, LAT), bf), vm((POOL, PAGE, LAT), bf), vm((2, LAT, PLEN), bf),
            vm((HEADS, KVL, VH), bf), vm((NX, COLS, DEPTH), bf), vm((REQ, 128), bf),
            vm((2 * REQ, COLS), bf), vm((REQ, 128), bf),
            vm((8, PAGE, LAT), bf), vm((128, PAGE, LAT), bf), vm((CH, HEADS, LAT), f32),
            vm((CH * 2 * PAGE, LAT), bf), vm((3, CH, HEADS, 128), jnp.int32), vm((ROWS, KVL), f32),
            vm((2, ROWS, 128), f32), vm((KVL // 128, ROWS, 128), f32),
            vm((CHUNKS, NZ * CH, DEPTH), bf), vm((CHUNKS, 2, NZ * CH, COLS), bf),
            vm((CHUNKS, 2, NZ * CH, COLS), bf), vm((CHUNKS, 2, NZ * CH, COLS), f32),
            vm((CHUNKS, 2, 4, 2, CH, COLS), bf), vm((CHUNKS, 2, 4, 2, CH, COLS), bf),
            vm((2, REQ, COLS), bf), vm((2, REQ, COLS), bf), vm((2, REQ, COLS), bf),
            pltpu.SemaphoreType.DMA((8,)),
            pltpu.SemaphoreType.DMA((SEMS,)),
            pltpu.SemaphoreType.DMA((SEMS,)),
        ],
        compiler_params=pltpu.CompilerParams(
            collective_id=0, has_side_effects=True, vmem_limit_bytes=60 * 1024 * 1024
        ),
        name="attention_block",
    )(
        perm, pages, prefix_id, lengths, prefix_len, leave.reshape(-1), arrive,
        queries, page_pool, prefix_cache.transpose(0, 2, 1), value_up, output_weight.T, order, residual,
    )
    new_pool = pl.pallas_call(
        place_pages,
        out_shape=jax.ShapeDtypeStruct((POOL, PAGE, LAT), bf),
        in_specs=[smem] * 2 + [hbm] * 2,
        out_specs=hbm,
        scratch_shapes=[vm((POOL, PAGE, LAT), bf), pltpu.SemaphoreType.DMA((3,))],
        compiler_params=pltpu.CompilerParams(vmem_limit_bytes=60 * 1024 * 1024),
        name="place_pages",
    )(pages, move_list[0].T.reshape(-1), page_pool, arr)
    return (layer_out, new_pool)


def solution(mesh):
    in_specs = (
        P("dp", "tp", None),
        P("dp", None, None),
        P(),
        P("dp", None),
        P("dp"),
        P("dp"),
        P(),
        P("dp", None, None),
        P("tp", None, None),
        P("tp", "dp"),
        P("tp", "dp"),
    )
    out_specs = (P("tp", "dp"), P("dp", None, None))
    return jax.shard_map(local, mesh=mesh, in_specs=in_specs, out_specs=out_specs, check_vma=False)
```

time: 330 us -> 105 us (0.32)
  waiting for transfers between devices: 184 us -> 0 us
  Pallas kernels: 0 us -> 95.1 us
  local copies, waits for them, and re-layouts: 79.7 us -> 5.75 us
  starting transfers between devices: 23.2 us -> 0 us
  matrix products: 18.8 us -> 0 us
  between operations: 14.3 us -> 0.7 us
  other arithmetic: 8.2 us -> 3.34 us
    pallas_call x0 -> x2, Pallas kernels: none -> 95.1 us  [the longest x1 89 us: local(): pl.pallas_call(fused, out_shape=(jax.ShapeDtypeStruct((2 * REQ, COLS), bf...]
    all_gather x1 -> x0, waiting for transfers between devices: 94.7 us -> none  [local(): lax.all_gather(heads_out, 'dp', axis=0, tiled=True)]
    reduce_scatter x1 -> x0, waiting for transfers between devices: 58.4 us -> none  [local(): lax.psum_scatter(partial_rows, 'tp', scatter_dimension=0, tiled=True)]
    scatter x3 -> x0, local copies, waits for them, and re-layouts: 45.1 us -> none  [the longest x1 25.3 us: local(): outgoing = jnp.zeros((rank_count, CAP, request_width), page_pool.dtype).a...]
    all_to_all x2 -> x0, waiting for transfers between devices: 30.8 us -> none  [the longest x1 30.8 us: local(): lax.all_to_all(outgoing, 'dp', split_axis=0, concat_axis=0, tiled=True)]
    all_to_all x2 -> x0, starting transfers between devices: 23 us -> none  [the longest x1 13.8 us: local(): lax.all_to_all(labels, 'dp', split_axis=0, concat_axis=0, tiled=True)]
    dot_general x5 -> x0, matrix products: 18.8 us -> none  [the longest x1 6.31 us: local(): jnp.dot(lax.all_gather(heads_out, 'dp', axis=0, tiled=True), output_weigh...]
    gather x5 -> x0, local copies, waits for them, and re-layouts: 9.54 us -> none  [the longest x1 5.39 us: local(): new_pool[page_table].reshape(requests, per_request * page_size, latent)]
  transfers between devices with their start and end apart: 4 -> 0, of which waited for: 3 -> 0; matrix products, arithmetic and copies ran while one was open for 17% -> 0% of each run, Pallas kernels for 0% -> 0%
where the time goes in v1:
time: 105 us
  Pallas kernels  95.1 us (91%)
  local copies, waits for them, and re-layouts  5.75 us (5%)
  other arithmetic  3.34 us (3%)
    pallas_call x1, Pallas kernels, local(): pl.pallas_call(fused, out_shape=(jax.ShapeDtypeStruct((2 * REQ, COLS), bf...  89 us
    pallas_call x1, Pallas kernels, local(): pl.pallas_call(place_pages, out_shape=jax.ShapeDtypeStruct((POOL, PAGE, L...  6.13 us

profile of v1, /device:TPU:1, one launch (start us, length us, event | category | flops | bytes accessed | tf_op | source)
XLA Modules:
  0.0 104.9 jit_solution(16421147614052875045)
XLA Ops:
  0.6 0.7 slice_bitcast_fusion
  1.3 0.1 select_reduce_fusion.4
  1.4 0.7 fusion.4
  2.1 0.1 slice.11
  2.2 1.4 %reshape.150.page_s = s32[192]{0:T(256)} reshape(s32[2,96]{1,0:T(2,128)} %bitcast.18) | data formatting | bytes 1536 | tf_op jit(solution)/shard_map/reshape | solution.py:532
  3.5 0.1 iota_compare_fusion.4
  3.6 0.7 copy.19
  4.3 0.7 reshape.153.move_s
  5.0 0.1 iota_compare_fusion.3
  5.1 0.8 select_reduce_fusion.3
  5.9 0.1 select_reduce_fusion.1
  6.0 0.6 select_reduce_fusion.perm_s
  6.6 0.1 reshape.151
  6.7 0.1 copy.15
  6.8 0.1 select_reduce_fusion.2
  6.9 0.1 multiply_add_fusion
  7.0 0.6 add.115.arrive_s
  7.6 0.7 fusion.1.order_h
  8.3 0.1 copy.16
  8.4 0.7 reshape.152.leave_s
  9.1 89.0 %attention_block.1 = (bf16[192,224]{1,0:T(8,128)(2,1)}, bf16[128,16,576]{2,1,0:T(8,128)(2,1)}) custom-call(s32[96]{0:T(128)} %select_reduce_fusion.perm_s, s32[192]{0:T(256)} %reshape.150.page_s, s32[96]{0:T(128)} %prefix_s.1, s32[96]{0:T(128)} %length_s.1, s32[2]{0:T(128)} %limit_s.1, s32[128]{0:T(128)} %reshape.152.leave_s, s32[64]{0:T(128)} %add.115.arrive_s, ...), custom_call_target="tpu_custom_call" | custom-call | tf_op jit(solution)/shard_map/attention_block/pallas_call | solution.py:539
  98.1 0.0 copy-start
  98.1 6.1 %place_pages.1 = bf16[192,16,576]{2,1,0:T(8,128)(2,1)} custom-call(s32[192]{0:T(256)} %reshape.150.page_s, s32[96]{0:T(128)} %reshape.153.move_s, bf16[192,16,576]{2,1,0:T(8,128)(2,1)} %pool_h.3, bf16[128,16,576]{2,1,0:T(8,128)(2,1)} %get-tuple-element.5.arr_h), custom_call_target="tpu_custom_call" | custom-call | tf_op jit(solution)/shard_map/place_pages/pallas_call | solution.py:570
  104.3 0.0 copy-done
  104.3 0.6 copy.21
  (3 shorter events, 0.0 us)
Async XLA Ops:
  98.1 6.1 %copy-start = (bf16[192,224]{1,0:T(8,128)(2,1)S(1)}, bf16[192,224]{1,0:T(8,128)(2,1)}, u32[]{:S(2)}) copy-start(bf16[192,224]{1,0:T(8,128)(2,1)} %get-tuple-element.12) | copy-start | bytes 258052

commit v2 on v1

v2 whole, which is shorter than its diff:
```python
import functools

import jax
import jax.numpy as jnp
from jax import lax
from jax.experimental import pallas as pl
from jax.experimental.pallas import tpu as pltpu
from jax.sharding import PartitionSpec as P

MESH = pl.DeviceIdType.MESH

LAT = 576
KVL = 512
HEADS = 8
VH = 128
PAGE = 16
REQ = 96
MOVES = 32
CH = 32
CHUNKS = REQ // CH
ROWS = CH * HEADS
POOL = 192
PLEN = 384
NZ, NX, NY = 8, 4, 8
COLS = 224
DEPTH = HEADS * VH
SCALE = 192.0 ** (-0.5)
MASKED = -1e30

NT = (((1,), (1,)), ((), ()))

W0 = 0
PD = W0 + 4
PY = PD + 8
PC = PY + 14
Z0 = PC + 15
CX = Z0 + 8 * CHUNKS
RS = CX + CHUNKS
OR = RS + 16 * CHUNKS
SEMS = OR + 16


def div(a, n):
    return lax.div(a, jnp.int32(n))


def rem(a, n):
    return lax.rem(a, jnp.int32(n))


def fused(
    page_s, prefix_s, length_s, limit_s,
    page_r, move_r,
    q_h, pool_h, kt_h, vup_h, wt_h, res_h,
    out_ref, come_o,
    q_v, pool_v, kt_v, vup_v, w_v, res_v, order_v, order_r,
    table_v, table_s,
    stage, arr, q_f, keys, rowinfo, blend, stats, merged,
    zb, sx, rx, own, ss, rr, red,
    lsem, ssem, rsem,
):
    d = lax.axis_index("dp")
    t = lax.axis_index("tp")
    z, x = div(d, NX), rem(d, NX)
    y, c = div(t, 2), rem(t, 2)
    kind, quarter = div(t, 4), rem(t, 4)

    def at_x(v):
        return (z * NX + rem(v + NX, NX), t)

    def at_z(v):
        return (rem(v + NZ, NZ) * NX + x, t)

    def at_y(v):
        return (d, rem(v + NY, NY) * 2 + c)

    def at_rank(v):
        return (rem(v + 32, 32), t)

    partner = (d, y * 2 + 1 - c)
    final_core = div(x, 2)
    diagonal = c == final_core

    sent = []

    def remote(src, dst, device, slot, recv_slot=None):
        return pltpu.make_async_remote_copy(
            src_ref=src, dst_ref=dst, send_sem=ssem.at[slot],
            recv_sem=rsem.at[slot if recv_slot is None else recv_slot],
            device_id=device, device_id_type=MESH,
        )

    def send(src, dst, device, slot):
        copy = remote(src, dst, device, slot)
        copy.start()
        sent.append(copy)

    def arrived(dst, slot):
        remote(dst, dst, partner, slot).wait_recv()

    def owner(core, e, s):
        return (z * NX + 2 * core + e, rem(y + s + NY, NY) * 2 + final_core)

    def itself(e):
        return diagonal & (2 * c + e == x)

    def order_itself(e):
        return (z == y) & (2 * c + e == x) & (rem(z, 2) == c)

    barrier = pltpu.get_barrier_semaphore()

    def greet(device):
        pl.semaphore_signal(barrier, inc=1, device_id=device, device_id_type=MESH)

    for i in range(8):
        offset = kind + 4 * i
        if i == 0:
            @pl.when(offset != 0)
            def _():
                greet(at_rank(d - offset))
        else:
            greet(at_rank(d - offset))
    for device in (
        at_x(x + 1), at_x(x - 1), at_z(z + 1), at_z(z - 1), at_z(z + 2), at_z(z - 2),
        at_y(y + 1), at_y(y - 1), partner,
    ):
        greet(device)
    for s in range(NY):
        for e in range(2):
            source = (z * NX + 2 * c + e, rem(y - s + NY, NY) * 2 + final_core)
            if s == 0:
                @pl.when(jnp.logical_not(itself(e)))
                def _():
                    greet(source)
            else:
                greet(source)
    for e in range(2):
        @pl.when(jnp.logical_not(order_itself(e)))
        def _():
            greet((y * NX + 2 * c + e, y * 2 + rem(z, 2)))

    loads = {}
    for n, (name, src, dst) in enumerate([
        ("pool", pool_h, pool_v), ("q", q_h, q_v), ("kt", kt_h, kt_v), ("vup", vup_h, vup_v),
        ("w", wt_h, w_v.at[x]), ("res", res_h, res_v),
    ]):
        loads[name] = pltpu.make_async_copy(src, dst, lsem.at[n])
        loads[name].start()

    def iota(shape, dim):
        return lax.broadcasted_iota(jnp.int32, shape, dim)

    def column_of(row, n):
        return jnp.sum(jnp.where(iota((n, n), 0) == iota((n, n), 1), row, 0), axis=1, keepdims=True)

    leaving = move_r[0]
    ahead_by = move_r[1] - d
    offsets = jnp.where(ahead_by < 0, ahead_by + 32, ahead_by)
    leaving_column = column_of(leaving, MOVES)
    offset_column = column_of(offsets, MOVES)
    is_left = iota((REQ, MOVES), 0) == leaving
    left = jnp.sum(jnp.where(is_left, 1, 0), axis=1, keepdims=True)
    move_of = jnp.sum(jnp.where(is_left, iota((REQ, MOVES), 1), 0), axis=1, keepdims=True)
    by_move = iota((MOVES, REQ), 1) == leaving_column
    left_row = jnp.sum(jnp.where(by_move, 1, 0), axis=0, keepdims=True)
    before = jnp.sum(
        jnp.where(iota((REQ, REQ), 1) < iota((REQ, REQ), 0), 1 - left_row, 0), axis=1, keepdims=True
    )
    position = jnp.where(left > 0, REQ - MOVES + move_of, before)
    placed = position == iota((REQ, 128), 1)
    order_v[...] = jnp.where(placed, 1.0, 0.0).astype(jnp.bfloat16)
    perm = jnp.sum(jnp.where(placed, iota((REQ, 128), 0), 0), axis=0, keepdims=True)
    table_v[0:1, :] = perm
    parity = lax.broadcasted_iota(jnp.int32, (MOVES, MOVES), 0) & 1
    for p in range(2):
        row = page_r[p:p + 1, :]
        moved_page = jnp.sum(jnp.where(by_move, row, 0), axis=1, keepdims=True)
        for b in range(2):
            hit = (offset_column == iota((MOVES, MOVES), 1)) & (parity == b)
            table_v[1 + 2 * b + p:2 + 2 * b + p, :MOVES] = jnp.sum(
                jnp.where(hit, moved_page, 0), axis=0, keepdims=True
            )
        b = lax.broadcasted_iota(jnp.int32, (1, MOVES), 1) & 1
        table_v[5 + p:6 + p, :MOVES] = (
            ((offsets & 3) * 4 + 2 * b + p) * 8 + lax.shift_right_logical(offsets, 2)
        )
    to_scalar = pltpu.make_async_copy(table_v, table_s, lsem.at[6])
    to_scalar.start()

    expected = 9 + jnp.where(kind == 0, 7, 8) + jnp.where(diagonal, 15, 16)
    expected = expected + jnp.where(z == y, jnp.where(diagonal & (rem(z, 2) == c), 15, 16), 0)
    pl.semaphore_wait(barrier, expected)
    to_scalar.wait()

    def listed(row, at, size):
        return jnp.clip(table_s[row, at], 0, size - 1)


    def weights():
        send(wt_h, w_v.at[x], at_x(x + 1), W0)
        send(wt_h, w_v.at[x], at_x(x - 1), W0 + 1)
        yield
        half = COLS // 2
        low, high = rem(x + NX - 1, NX), rem(x + 1, NX)
        arrived(w_v.at[low], W0)
        send(w_v.at[low, pl.ds(0, half)], w_v.at[low, pl.ds(0, half)], at_x(x + 1), W0 + 2)
        arrived(w_v.at[high], W0 + 1)
        send(w_v.at[high, pl.ds(half, half)], w_v.at[high, pl.ds(half, half)], at_x(x - 1), W0 + 3)
        yield
        far = rem(x + 2, NX)
        arrived(w_v.at[far, pl.ds(0, half)], W0 + 2)
        arrived(w_v.at[far, pl.ds(half, half)], W0 + 3)
        loads["w"].wait()
        yield

    def pages_out():
        loads["pool"].wait()
        for i in range(8):
            offset = kind + 4 * i
            stage[i] = pool_v[listed(1 + quarter, offset, POOL)]

            def go():
                remote(stage.at[i], arr.at[t * 8 + i], at_rank(d + offset), PD + i).start()
            if i == 0:
                pl.when(offset != 0)(go)

                @pl.when(offset == 0)
                def _():
                    arr[t * 8] = jnp.zeros((PAGE, LAT), arr.dtype)
            else:
                go()
        yield
        for i in range(8):
            def come():
                copy = remote(stage.at[i], arr.at[t * 8 + i], partner, PD + i)
                copy.wait_send()
                copy.wait_recv()
            if i == 0:
                pl.when(kind != 0)(come)
            else:
                come()

    def pages_ring():
        def part(o, half, core=c):
            return arr.at[pl.ds((o * 2 + core) * 8 + 4 * half, 4)]

        def block(o, core=c):
            return arr.at[pl.ds((o * 2 + core) * 8, 8)]

        devices = (at_y(y + 1), at_y(y - 1))
        for half in range(2):
            for way in range(2):
                send(part(y, half), part(y, half), devices[way], PY + 2 * half + way)
        send(block(y), block(y), partner, PC)
        yield
        for s in (1, 2, 3):
            for half in range(2):
                for way, o in ((0, rem(y + NY - s, NY)), (1, rem(y + s, NY))):
                    slot = 4 * (s - 1) + 2 * half + way
                    arrived(part(o, half), PY + slot)
                    if s < 3:
                        send(part(o, half), part(o, half), devices[way], PY + slot + 4)
                    elif half == way:
                        send(part(o, half), part(o, half), devices[way], PY + 12 + way)
                    send(part(o, half), part(o, half), partner, PC + 1 + slot)
                yield
        far = rem(y + 4, NY)
        for half in range(2):
            arrived(part(far, half), PY + 12 + half)
            send(part(far, half), part(far, half), partner, PC + 13 + half)
        other = 1 - c
        arrived(block(y, other), PC)
        for s in (1, 2, 3):
            for half in range(2):
                for way, o in ((0, rem(y + NY - s, NY)), (1, rem(y + s, NY))):
                    arrived(part(o, half, other), PC + 1 + 4 * (s - 1) + 2 * half + way)
        for half in range(2):
            arrived(part(far, half, other), PC + 13 + half)
        yield

    def prefix_part(n):
        def place(j, _):
            slot = listed(0, n * CH + j, REQ)
            q_f[j] = q_v[slot].astype(jnp.float32)
            prefix = prefix_s[slot]
            rowinfo[0, j] = jnp.full((HEADS, 128), prefix, jnp.int32)
            rowinfo[1, j] = jnp.full((HEADS, 128), limit_s[prefix], jnp.int32)
            rowinfo[2, j] = jnp.full((HEADS, 128), length_s[slot], jnp.int32)
            return 0

        lax.fori_loop(0, CH, place, 0)
        q = q_f[...].reshape(ROWS, LAT).astype(jnp.bfloat16)
        which = rowinfo[0].reshape(ROWS, 128)[:, :1] == 0
        limit = rowinfo[1].reshape(ROWS, 128)[:, :1]
        scores = jnp.where(
            which,
            jnp.dot(q, kt_v[0], preferred_element_type=jnp.float32),
            jnp.dot(q, kt_v[1], preferred_element_type=jnp.float32),
        ) * SCALE
        column = lax.broadcasted_iota(jnp.int32, (ROWS, PLEN), 1)
        scores = jnp.where(column < limit, scores, MASKED)
        highest = jnp.max(scores, axis=1, keepdims=True)
        raised = jnp.exp(scores - highest)
        total = jnp.sum(raised, axis=1, keepdims=True)
        stats[0] = jnp.broadcast_to(highest, (ROWS, 128))
        stats[1] = jnp.broadcast_to(total, (ROWS, 128))
        blend[...] = lax.dot_general(
            jnp.where(which, raised, 0.0).astype(jnp.bfloat16), kt_v[0, :KVL, :], NT,
            preferred_element_type=jnp.float32,
        ) + lax.dot_general(
            jnp.where(which, 0.0, raised).astype(jnp.bfloat16), kt_v[1, :KVL, :], NT,
            preferred_element_type=jnp.float32,
        )

    def own_part(n):
        def place(j, _):
            at = pl.multiple_of(j * 2 * PAGE, 2 * PAGE)
            if n < CHUNKS - 1:
                slot = listed(0, n * CH + j, REQ)
                keys[pl.ds(at, PAGE), :] = pool_v[page_s[0, slot]]
                keys[pl.ds(at + PAGE, PAGE), :] = pool_v[page_s[1, slot]]
            else:
                keys[pl.ds(at, PAGE), :] = arr[listed(5, j, 128)]
                keys[pl.ds(at + PAGE, PAGE), :] = arr[listed(6, j, 128)]
            return 0

        lax.fori_loop(0, CH, place, 0)
        if n == CHUNKS - 1:
            loads["come"] = pltpu.make_async_copy(keys, come_o, lsem.at[7])
            loads["come"].start()
        group = 64
        row = lax.broadcasted_iota(jnp.int32, (group, 256), 0)
        column = lax.broadcasted_iota(jnp.int32, (group, 256), 1)
        same = lax.shift_right_logical(row, 3) == lax.shift_right_logical(column, 5)
        token = column & 31
        for g in range(ROWS // group):
            rows = pl.ds(g * group, group)
            q = q_f[pl.ds(g * 8, 8)].reshape(group, LAT).astype(jnp.bfloat16)
            k = keys[pl.ds(g * 256, 256), :]
            length = rowinfo[2, pl.ds(g * 8, 8)].reshape(group, 128)[:, :1]
            scores = lax.dot_general(q, k, NT, preferred_element_type=jnp.float32) * SCALE
            scores = jnp.where(same & (token < length), scores, MASKED)
            high_own = jnp.max(scores, axis=1, keepdims=True)
            raised = jnp.exp(scores - high_own)
            total_own = jnp.sum(raised, axis=1, keepdims=True)
            blend_own = jnp.dot(
                raised.astype(jnp.bfloat16), keys[pl.ds(g * 256, 256), :KVL], preferred_element_type=jnp.float32
            )
            high_pre = stats[0, rows, :][:, :1]
            total_pre = stats[1, rows, :][:, :1]
            ceiling = jnp.maximum(high_pre, high_own)
            f = jnp.exp(high_pre - ceiling)
            h = jnp.exp(high_own - ceiling)
            mixed = (f * blend[rows, :] + h * blend_own) / (f * total_pre + h * total_own)
            for l in range(KVL // 128):
                merged[l, rows, :] = mixed[:, l * 128:(l + 1) * 128]
        mine = pl.ds(pl.multiple_of(z * CH, CH), CH)
        for h in range(HEADS):
            a = jnp.concatenate(
                [merged[l, pl.ds(h, CH, stride=HEADS), :] for l in range(KVL // 128)], axis=1
            ).astype(jnp.bfloat16)
            zb[n, mine, h * VH:(h + 1) * VH] = jnp.dot(
                a, vup_v[h], preferred_element_type=jnp.float32
            ).astype(jnp.bfloat16)

    def heads(n):
        def block(o):
            return zb.at[n, pl.ds(pl.multiple_of(o * CH, CH), CH)]

        def half(o, i):
            return zb.at[n, pl.ds(pl.multiple_of(o * CH + i * (CH // 2), CH // 2), CH // 2)]

        base = Z0 + 8 * n
        low = [rem(z + NZ - s, NZ) for s in range(4)]
        high = [rem(z + s, NZ) for s in range(5)]
        for s in (2, 1):
            send(block(z), block(z), at_z(z + s), base + 2 * s - 2)
            send(block(z), block(z), at_z(z - s), base + 2 * s - 1)
        yield
        arrived(block(low[2]), base + 2)
        send(block(low[2]), block(low[2]), at_z(z + 1), base + 4)
        send(half(low[2], 0), half(low[2], 0), at_z(z + 2), base + 6)
        arrived(block(high[2]), base + 3)
        send(block(high[2]), block(high[2]), at_z(z - 1), base + 5)
        send(half(high[2], 1), half(high[2], 1), at_z(z - 2), base + 7)
        yield
        arrived(block(low[1]), base)
        arrived(block(high[1]), base + 1)
        arrived(block(low[3]), base + 4)
        arrived(block(high[3]), base + 5)
        arrived(half(high[4], 0), base + 6)
        arrived(half(high[4], 1), base + 7)
        yield

    def product(n):
        for i in range(2):
            sx[n, i] = lax.dot_general(
                zb[n], w_v[2 * (1 - c) + i], NT, preferred_element_type=jnp.float32
            ).astype(jnp.bfloat16)
        send(sx.at[n], rx.at[n], partner, CX + n)
        for i in range(2):
            own[n, i] = lax.dot_general(zb[n], w_v[2 * c + i], NT, preferred_element_type=jnp.float32)

    def sums(n):
        base = RS + 16 * n
        arrived(rx.at[n], CX + n)
        for i in range(2):
            ss[n, i] = (own[n, i] + rx[n, i].astype(jnp.float32)).astype(jnp.bfloat16)
        mine = rem(x, 2)
        for s in (4, 3, 5, 2, 6, 1, 7, 0):
            rows = pl.ds(pl.multiple_of(rem(y + s, NY) * CH, CH), CH)
            for i in range(2):
                copy = remote(
                    ss.at[n, i, rows], rr.at[n, s, mine], owner(c, i, s), base + 2 * s + i, base + 2 * s + mine
                )
                if s == 0:
                    pl.when(jnp.logical_not(itself(i)))(copy.start)

                    @pl.when(itself(i))
                    def _():
                        rr[n, 0, mine] = ss[n, i, rows, :]
                else:
                    copy.start()
                    sent.append(copy)
        yield
        for e in range(2):
            total = None
            for s in (0, 1, 7, 2, 6, 3, 5, 4):
                copy = remote(rr.at[n, s, e], rr.at[n, s, e], partner, base + 2 * s + e)
                if s == 0:
                    pl.when(jnp.logical_not(itself(e)))(copy.wait_recv)
                else:
                    copy.wait_recv()
                part = rr[n, s, e].astype(jnp.float32)
                total = part if total is None else total + part
            red[e, n * CH:(n + 1) * CH] = total
        rows = pl.ds(0, CH)
        for i in range(2):
            copy = remote(ss.at[n, i, rows], ss.at[n, i, rows], partner, base + i)
            pl.when(jnp.logical_not(itself(i)))(copy.wait_send)
        yield

    def order_copies(act):
        mine = rem(x, 2)
        for a in range(4):
            for column in range(NX):
                to = (2 * a + c) * NX + column
                copy = remote(
                    order_v, order_r.at[mine], (to, y * 2 + final_core), OR + 4 * a + column, OR + mine
                )
                pl.when((z == y) & jnp.logical_not(diagonal & (to == d)))(functools.partial(act, copy))

    def order_send():
        order_copies(lambda copy: copy.start())

        @pl.when((z == y) & diagonal & (rem(z, 2) == c))
        def _():
            order_r[rem(x, 2)] = order_v[...]

    def order_wait():
        order_copies(lambda copy: copy.wait_send())
        for e in range(2):
            copy = remote(order_v, order_r.at[e], partner, OR + e)
            pl.when(jnp.logical_not(order_itself(e)))(copy.wait_recv)

    def finish():
        loads["res"].wait()
        for e in range(2):
            place = order_r[e][:, :REQ]
            rows = pl.ds(e * REQ, REQ)
            total = red[e]
            high = total.astype(jnp.bfloat16)
            low = (total - high.astype(jnp.float32)).astype(jnp.bfloat16)
            placed = jnp.dot(place, high, preferred_element_type=jnp.float32) + jnp.dot(
                place, low, preferred_element_type=jnp.float32
            )
            out_ref[rows, :] = (res_v[rows, :].astype(jnp.float32) + placed).astype(jnp.bfloat16)

    w = weights()
    p = pages_out()
    r = pages_ring()
    hs = [heads(n) for n in range(CHUNKS)]
    rs = [sums(n) for n in range(CHUNKS)]

    next(p)
    next(w)
    order_send()
    loads["q"].wait()
    loads["kt"].wait()
    prefix_part(0)
    loads["vup"].wait()
    own_part(0)
    next(hs[0])
    next(p, None)
    next(r)
    prefix_part(1)
    own_part(1)
    next(hs[1])
    next(r)
    next(r)
    next(hs[0])
    next(w)
    next(r)
    next(r)
    prefix_part(2)
    next(hs[1])
    next(r)
    next(r)
    next(w)
    next(r)
    own_part(2)
    next(hs[2])
    next(hs[0])
    product(0)
    next(rs[0])
    next(hs[2])
    next(hs[1])
    product(1)
    next(rs[1])
    next(rs[0])
    order_wait()
    next(hs[2])
    product(2)
    next(rs[1])
    next(rs[2])
    next(rs[2])
    finish()
    for copy in sent:
        copy.wait_send()
    loads["come"].wait()


PARTS = 4


def place_pages(page_s, move_s, pool_h, come_h, new_h, pool_v, come_v, sem):
    size = POOL // PARTS
    come = pltpu.make_async_copy(come_h, come_v, sem.at[2 * PARTS])
    come.start()
    parts = [pl.ds(n * size, size) for n in range(PARTS)]
    loads = [pltpu.make_async_copy(pool_h.at[part], pool_v.at[part], sem.at[n]) for n, part in enumerate(parts)]
    stores = [pltpu.make_async_copy(pool_v.at[part], new_h.at[part], sem.at[PARTS + n]) for n, part in enumerate(parts)]
    for load in loads:
        load.start()
    come.wait()
    for n in range(PARTS):
        loads[n].wait()

        def place(k, _):
            slot = move_s[0, 0, k]
            for p in range(2):
                page = page_s[p, slot]

                @pl.when((page >= n * size) & (page < (n + 1) * size))
                def _():
                    pool_v[page] = come_v[2 * k + p]
            return 0

        lax.fori_loop(0, MOVES, place, 0)
        stores[n].start()
    for store in stores:
        store.wait()


def local(
    queries, page_pool, prefix_cache, page_table, lengths, prefix_id, prefix_len,
    move_list, value_up, output_weight, residual,
):
    pages = page_table.T
    moves = move_list.transpose(2, 0, 1)
    smem = pl.BlockSpec(memory_space=pltpu.SMEM)
    vmem = pl.BlockSpec(memory_space=pltpu.VMEM)
    hbm = pl.BlockSpec(memory_space=pl.ANY)
    bf, f32 = jnp.bfloat16, jnp.float32
    vm = pltpu.VMEM
    layer_out, come = pl.pallas_call(
        fused,
        out_shape=(
            jax.ShapeDtypeStruct((2 * REQ, COLS), bf),
            jax.ShapeDtypeStruct((CH * 2 * PAGE, LAT), bf),
        ),
        in_specs=[smem] * 4 + [vmem] * 2 + [hbm] * 6,
        out_specs=(vmem, hbm),
        scratch_shapes=[
            vm((REQ, HEADS, LAT), bf), vm((POOL, PAGE, LAT), bf), vm((2, LAT, PLEN), bf),
            vm((HEADS, KVL, VH), bf), vm((NX, COLS, DEPTH), bf), vm((2 * REQ, COLS), bf),
            vm((REQ, 128), bf), vm((2, REQ, 128), bf),
            vm((8, 128), jnp.int32), pltpu.SMEM((8, 128), jnp.int32),
            vm((8, PAGE, LAT), bf), vm((128, PAGE, LAT), bf), vm((CH, HEADS, LAT), f32),
            vm((CH * 2 * PAGE, LAT), bf), vm((3, CH, HEADS, 128), jnp.int32), vm((ROWS, KVL), f32),
            vm((2, ROWS, 128), f32), vm((KVL // 128, ROWS, 128), f32),
            vm((CHUNKS, NZ * CH, DEPTH), bf), vm((CHUNKS, 2, NZ * CH, COLS), bf),
            vm((CHUNKS, 2, NZ * CH, COLS), bf), vm((CHUNKS, 2, NZ * CH, COLS), f32),
            vm((CHUNKS, 2, NZ * CH, COLS), bf), vm((CHUNKS, NY, 2, CH, COLS), bf),
            vm((2, REQ, COLS), f32),
            pltpu.SemaphoreType.DMA((8,)),
            pltpu.SemaphoreType.DMA((SEMS,)),
            pltpu.SemaphoreType.DMA((SEMS,)),
        ],
        compiler_params=pltpu.CompilerParams(
            collective_id=0, has_side_effects=True, vmem_limit_bytes=60 * 1024 * 1024
        ),
        name="attention_block",
    )(
        pages, prefix_id, lengths, prefix_len, pages, moves,
        queries, page_pool, prefix_cache.transpose(0, 2, 1), value_up, output_weight.T, residual,
    )
    new_pool = pl.pallas_call(
        place_pages,
        out_shape=jax.ShapeDtypeStruct((POOL, PAGE, LAT), bf),
        in_specs=[smem] * 2 + [hbm] * 2,
        out_specs=hbm,
        scratch_shapes=[
            vm((POOL, PAGE, LAT), bf), vm((2 * MOVES, PAGE, LAT), bf), pltpu.SemaphoreType.DMA((2 * PARTS + 1,))
        ],
        compiler_params=pltpu.CompilerParams(vmem_limit_bytes=60 * 1024 * 1024),
        name="place_pages",
    )(pages, moves, page_pool, come.reshape(2 * MOVES, PAGE, LAT))
    return (layer_out, new_pool)


def solution(mesh):
    in_specs = (
        P("dp", "tp", None),
        P("dp", None, None),
        P(),
        P("dp", None),
        P("dp"),
        P("dp"),
        P(),
        P("dp", None, None),
        P("tp", None, None),
        P("tp", "dp"),
        P("tp", "dp"),
    )
    out_specs = (P("tp", "dp"), P("dp", None, None))
    return jax.shard_map(local, mesh=mesh, in_specs=in_specs, out_specs=out_specs, check_vma=False)
```

time: 105 us -> 81.5 us (0.78)
  Pallas kernels: 95.1 us -> 80 us
  local copies, waits for them, and re-layouts: 5.75 us -> 0.65 us
  other arithmetic: 3.34 us -> 0 us
    pallas_call x1, Pallas kernels: 89 us -> 73.1 us  [local(): pl.pallas_call(fused, out_shape=(jax.ShapeDtypeStruct((2 * REQ, COLS), bf...]
    reshape x4 -> x0, local copies, waits for them, and re-layouts: 2.84 us -> none  [the longest x1 1.36 us: local(): pages = pages.reshape(-1)]
    reduce_sum x5 -> x0, other arithmetic: 1.72 us -> none  [the longest x1 0.79 us: local(): jnp.sum(jnp.where(is_left[None, :, :], pages[:, :, None], 0), axis=1)]
where the time goes in v2:
time: 81.5 us; the launch traced here: 81.3 us
  Pallas kernels  80 us (98%)
    pallas_call x1, Pallas kernels, local(): pl.pallas_call(fused, out_shape=(jax.ShapeDtypeStruct((2 * REQ, COLS), bf...  73.1 us
    pallas_call x1, Pallas kernels, local(): pl.pallas_call(place_pages, out_shape=jax.ShapeDtypeStruct((POOL, PAGE, L...  6.95 us

profile of v2, /device:TPU:1, one launch (start us, length us, event | category | flops | bytes accessed | tf_op | source)
XLA Modules:
  0.0 81.3 jit_solution(6933693407808624043)
XLA Ops:
  0.6 73.1 %attention_block.1 = (bf16[192,224]{1,0:T(8,128)(2,1)}, bf16[1024,576]{1,0:T(8,128)(2,1)}) custom-call(s32[2,96]{1,0:T(2,128)} %bitcast.8, s32[96]{0:T(128)} %prefix_s.1, s32[96]{0:T(128)} %length_s.1, s32[2]{0:T(128)} %limit_s.1, s32[2,96]{1,0:T(2,128)} %bitcast.9, s32[3,1,32]{2,1,0:T(1,128)} %bitcast.11, bf16[96,8,576]{2,1,0:T(8,128)(2,1)} %q_h.1, ...), custom_call_target="tpu_custom_call" | custom-call | tf_op jit(solution)/shard_map/attention_block/pallas_call | solution.py:576
  73.7 0.0 copy-start
  73.7 6.9 %place_pages.1 = bf16[192,16,576]{2,1,0:T(8,128)(2,1)} custom-call(s32[2,96]{1,0:T(2,128)} %bitcast.10, s32[3,1,32]{2,1,0:T(1,128)} %bitcast.12, bf16[192,16,576]{2,1,0:T(8,128)(2,1)} %pool_h.3, bf16[64,16,576]{2,1,0:T(8,128)(2,1)} %bitcast.5), custom_call_target="tpu_custom_call" | custom-call | tf_op jit(solution)/shard_map/place_pages/pallas_call | solution.py:608
  80.7 0.0 copy-done
  80.7 0.6 copy.14
Async XLA Ops:
  73.7 7.0 %copy-start = (bf16[192,224]{1,0:T(8,128)(2,1)S(1)}, bf16[192,224]{1,0:T(8,128)(2,1)}, u32[]{:S(2)}) copy-start(bf16[192,224]{1,0:T(8,128)(2,1)} %get-tuple-element.8) | copy-start | bytes 258052

commit v3 on v2

--- a/solution.py
+++ b/solution.py
@@ -27,16 +27,23 @@
 SCALE = 192.0 ** (-0.5)
 MASKED = -1e30
 
+PLAN = (
+    "p", "w", "a0", "b0", "h0", "r", "a1", "b1", "h1", "o", "r", "h0", "w", "r", "a2", "h1", "r", "w",
+    "h0", "m0", "r", "b2", "h2", "s0", "h1", "m1", "h2", "s1", "s0", "n", "s1", "O", "h2", "m2", "s2",
+    "s0", "s2", "s1", "s2",
+)
+
 NT = (((1,), (1,)), ((), ()))
 
 W0 = 0
 PD = W0 + 4
 PY = PD + 8
-PC = PY + 14
-Z0 = PC + 15
+PC = PY + 28
+Z0 = PC + 8
 CX = Z0 + 8 * CHUNKS
-RS = CX + CHUNKS
-OR = RS + 16 * CHUNKS
+RS = CX + 2 * CHUNKS
+RL = RS + 16 * CHUNKS
+OR = RL + CHUNKS
 SEMS = OR + 16
 
 
@@ -52,11 +59,11 @@
     page_s, prefix_s, length_s, limit_s,
     page_r, move_r,
     q_h, pool_h, kt_h, vup_h, wt_h, res_h,
-    out_ref, come_o,
-    q_v, pool_v, kt_v, vup_v, w_v, res_v, order_v, order_r,
+    out_ref, pool_o,
+    q_v, big, kt_v, vup_v, w_v, res_v, order_v, order_r,
     table_v, table_s,
     stage, arr, q_f, keys, rowinfo, blend, stats, merged,
-    zb, sx, rx, own, ss, rr, red,
+    zb, sx, rx, own, ss, rr, relay, red, new,
     lsem, ssem, rsem,
 ):
     d = lax.axis_index("dp")
@@ -106,6 +113,14 @@
 
     def order_itself(e):
         return (z == y) & (2 * c + e == x) & (rem(z, 2) == c)
+
+    loads = {}
+    for n, (name, src, dst) in enumerate([
+        ("pool", pool_h, big.at[pl.ds(0, POOL)]), ("q", q_h, q_v), ("kt", kt_h, kt_v), ("vup", vup_h, vup_v),
+        ("w", wt_h, w_v.at[x]), ("res", res_h, res_v),
+    ]):
+        loads[name] = pltpu.make_async_copy(src, dst, lsem.at[n])
+        loads[name].start()
 
     barrier = pltpu.get_barrier_semaphore()
 
@@ -122,7 +137,7 @@
             greet(at_rank(d - offset))
     for device in (
         at_x(x + 1), at_x(x - 1), at_z(z + 1), at_z(z - 1), at_z(z + 2), at_z(z - 2),
-        at_y(y + 1), at_y(y - 1), partner,
+        at_y(y + 1), at_y(y - 1), at_y(y + 2), partner,
     ):
         greet(device)
     for s in range(NY):
@@ -138,14 +153,6 @@
         @pl.when(jnp.logical_not(order_itself(e)))
         def _():
             greet((y * NX + 2 * c + e, y * 2 + rem(z, 2)))
-
-    loads = {}
-    for n, (name, src, dst) in enumerate([
-        ("pool", pool_h, pool_v), ("q", q_h, q_v), ("kt", kt_h, kt_v), ("vup", vup_h, vup_v),
-        ("w", wt_h, w_v.at[x]), ("res", res_h, res_v),
-    ]):
-        loads[name] = pltpu.make_async_copy(src, dst, lsem.at[n])
-        loads[name].start()
 
     def iota(shape, dim):
         return lax.broadcasted_iota(jnp.int32, shape, dim)
@@ -172,6 +179,7 @@
     perm = jnp.sum(jnp.where(placed, iota((REQ, 128), 0), 0), axis=0, keepdims=True)
     table_v[0:1, :] = perm
     parity = lax.broadcasted_iota(jnp.int32, (MOVES, MOVES), 0) & 1
+    sources = [0, 0]
     for p in range(2):
         row = page_r[p:p + 1, :]
         moved_page = jnp.sum(jnp.where(by_move, row, 0), axis=1, keepdims=True)
@@ -180,14 +188,25 @@
             table_v[1 + 2 * b + p:2 + 2 * b + p, :MOVES] = jnp.sum(
                 jnp.where(hit, moved_page, 0), axis=0, keepdims=True
             )
+        for half in range(2):
+            sources[half] += jnp.sum(
+                jnp.where(
+                    moved_page == iota((MOVES, 128), 1) + 128 * half, POOL + 2 * iota((MOVES, 128), 0) + p, 0
+                ),
+                axis=0, keepdims=True,
+            )
         b = lax.broadcasted_iota(jnp.int32, (1, MOVES), 1) & 1
         table_v[5 + p:6 + p, :MOVES] = (
             ((offsets & 3) * 4 + 2 * b + p) * 8 + lax.shift_right_logical(offsets, 2)
         )
+    for half in range(2):
+        table_v[8 + half:9 + half, :] = jnp.where(
+            sources[half] > 0, sources[half], iota((1, 128), 1) + 128 * half
+        )
     to_scalar = pltpu.make_async_copy(table_v, table_s, lsem.at[6])
     to_scalar.start()
 
-    expected = 9 + jnp.where(kind == 0, 7, 8) + jnp.where(diagonal, 15, 16)
+    expected = 10 + jnp.where(kind == 0, 7, 8) + jnp.where(diagonal, 15, 16)
     expected = expected + jnp.where(z == y, jnp.where(diagonal & (rem(z, 2) == c), 15, 16), 0)
     pl.semaphore_wait(barrier, expected)
     to_scalar.wait()
@@ -217,7 +236,7 @@
         loads["pool"].wait()
         for i in range(8):
             offset = kind + 4 * i
-            stage[i] = pool_v[listed(1 + quarter, offset, POOL)]
+            stage[i] = big[listed(1 + quarter, offset, POOL)]
 
             def go():
                 remote(stage.at[i], arr.at[t * 8 + i], at_rank(d + offset), PD + i).start()
@@ -230,55 +249,64 @@
             else:
                 go()
         yield
-        for i in range(8):
-            def come():
-                copy = remote(stage.at[i], arr.at[t * 8 + i], partner, PD + i)
-                copy.wait_send()
-                copy.wait_recv()
-            if i == 0:
-                pl.when(kind != 0)(come)
-            else:
-                come()
+
+    def page_come(i):
+        def come():
+            copy = remote(stage.at[i], arr.at[t * 8 + i], partner, PD + i)
+            copy.wait_send()
+            copy.wait_recv()
+        if i == 0:
+            pl.when(kind != 0)(come)
+        else:
+            come()
 
     def pages_ring():
-        def part(o, half, core=c):
-            return arr.at[pl.ds((o * 2 + core) * 8 + 4 * half, 4)]
+        parts = 4
+
+        def part(o, k, core=c):
+            return arr.at[pl.ds((o * 2 + core) * 8 + (8 // parts) * k, 8 // parts)]
 
         def block(o, core=c):
             return arr.at[pl.ds((o * 2 + core) * 8, 8)]
 
         devices = (at_y(y + 1), at_y(y - 1))
-        for half in range(2):
+        for k in range(parts):
+            for i in range(8 // parts):
+                page_come(k * (8 // parts) + i)
             for way in range(2):
-                send(part(y, half), part(y, half), devices[way], PY + 2 * half + way)
+                send(part(y, k), part(y, k), devices[way], PY + 2 * k + way)
         send(block(y), block(y), partner, PC)
         yield
         for s in (1, 2, 3):
-            for half in range(2):
-                for way, o in ((0, rem(y + NY - s, NY)), (1, rem(y + s, NY))):
-                    slot = 4 * (s - 1) + 2 * half + way
-                    arrived(part(o, half), PY + slot)
+            sides = ((0, rem(y + NY - s, NY)), (1, rem(y + s, NY)))
+            for k in range(parts):
+                for way, o in sides:
+                    slot = PY + 2 * parts * (s - 1) + 2 * k + way
+                    arrived(part(o, k), slot)
                     if s < 3:
-                        send(part(o, half), part(o, half), devices[way], PY + slot + 4)
-                    elif half == way:
-                        send(part(o, half), part(o, half), devices[way], PY + 12 + way)
-                    send(part(o, half), part(o, half), partner, PC + 1 + slot)
-                yield
+                        send(part(o, k), part(o, k), devices[way], slot + 2 * parts)
+                    elif k // (parts // 2) == way:
+                        send(part(o, k), part(o, k), devices[way], PY + 6 * parts + k)
+            for way, o in sides:
+                send(block(o), block(o), partner, PC + 2 * s - 1 + way)
+            yield
         far = rem(y + 4, NY)
-        for half in range(2):
-            arrived(part(far, half), PY + 12 + half)
-            send(part(far, half), part(far, half), partner, PC + 13 + half)
+        for k in range(parts):
+            arrived(part(far, k), PY + 6 * parts + k)
+        send(block(far), block(far), partner, PC + 7)
         other = 1 - c
         arrived(block(y, other), PC)
         for s in (1, 2, 3):
-            for half in range(2):
-                for way, o in ((0, rem(y + NY - s, NY)), (1, rem(y + s, NY))):
-                    arrived(part(o, half, other), PC + 1 + 4 * (s - 1) + 2 * half + way)
-        for half in range(2):
-            arrived(part(far, half, other), PC + 13 + half)
+            for way, o in ((0, rem(y + NY - s, NY)), (1, rem(y + s, NY))):
+                arrived(block(o, other), PC + 2 * s - 1 + way)
+        arrived(block(far, other), PC + 7)
         yield
 
     def prefix_part(n):
+        if n == 0:
+            loads["q"].wait()
+            loads["kt"].wait()
+
         def place(j, _):
             slot = listed(0, n * CH + j, REQ)
             q_f[j] = q_v[slot].astype(jnp.float32)
@@ -288,7 +316,7 @@
             rowinfo[2, j] = jnp.full((HEADS, 128), length_s[slot], jnp.int32)
             return 0
 
-        lax.fori_loop(0, CH, place, 0)
+        lax.fori_loop(0, CH, place, 0, unroll=4)
         q = q_f[...].reshape(ROWS, LAT).astype(jnp.bfloat16)
         which = rowinfo[0].reshape(ROWS, 128)[:, :1] == 0
         limit = rowinfo[1].reshape(ROWS, 128)[:, :1]
@@ -313,21 +341,20 @@
         )
 
     def own_part(n):
+        if n == 0:
+            loads["vup"].wait()
+
         def place(j, _):
-            at = pl.multiple_of(j * 2 * PAGE, 2 * PAGE)
             if n < CHUNKS - 1:
                 slot = listed(0, n * CH + j, REQ)
-                keys[pl.ds(at, PAGE), :] = pool_v[page_s[0, slot]]
-                keys[pl.ds(at + PAGE, PAGE), :] = pool_v[page_s[1, slot]]
+                keys[2 * j] = big[page_s[0, slot]]
+                keys[2 * j + 1] = big[page_s[1, slot]]
             else:
-                keys[pl.ds(at, PAGE), :] = arr[listed(5, j, 128)]
-                keys[pl.ds(at + PAGE, PAGE), :] = arr[listed(6, j, 128)]
+                big[POOL + 2 * j] = arr[listed(5, j, 128)]
+                big[POOL + 2 * j + 1] = arr[listed(6, j, 128)]
             return 0
 
-        lax.fori_loop(0, CH, place, 0)
-        if n == CHUNKS - 1:
-            loads["come"] = pltpu.make_async_copy(keys, come_o, lsem.at[7])
-            loads["come"].start()
+        lax.fori_loop(0, CH, place, 0, unroll=4)
         group = 64
         row = lax.broadcasted_iota(jnp.int32, (group, 256), 0)
         column = lax.broadcasted_iota(jnp.int32, (group, 256), 1)
@@ -336,7 +363,8 @@
         for g in range(ROWS // group):
             rows = pl.ds(g * group, group)
             q = q_f[pl.ds(g * 8, 8)].reshape(group, LAT).astype(jnp.bfloat16)
-            k = keys[pl.ds(g * 256, 256), :]
+            pages = pl.ds(g * 16, 16) if n < CHUNKS - 1 else pl.ds(POOL + g * 16, 16)
+            k = (keys if n < CHUNKS - 1 else big)[pages].reshape(256, LAT)
             length = rowinfo[2, pl.ds(g * 8, 8)].reshape(group, 128)[:, :1]
             scores = lax.dot_general(q, k, NT, preferred_element_type=jnp.float32) * SCALE
             scores = jnp.where(same & (token < length), scores, MASKED)
@@ -344,7 +372,7 @@
             raised = jnp.exp(scores - high_own)
             total_own = jnp.sum(raised, axis=1, keepdims=True)
             blend_own = jnp.dot(
-                raised.astype(jnp.bfloat16), keys[pl.ds(g * 256, 256), :KVL], preferred_element_type=jnp.float32
+                raised.astype(jnp.bfloat16), k[:, :KVL], preferred_element_type=jnp.float32
             )
             high_pre = stats[0, rows, :][:, :1]
             total_pre = stats[1, rows, :][:, :1]
@@ -363,6 +391,17 @@
                 a, vup_v[h], preferred_element_type=jnp.float32
             ).astype(jnp.bfloat16)
 
+    def new_pool():
+        def place(i, row):
+            new[128 * row + i] = big[listed(8 + row, i, POOL + 2 * MOVES)]
+            return row
+
+        for n, (row, count) in enumerate(((0, 128), (1, POOL - 128))):
+            lax.fori_loop(0, count, place, row, unroll=4)
+            part = pl.ds(128 * row, count)
+            loads[f"new{row}"] = pltpu.make_async_copy(new.at[part], pool_o.at[part], lsem.at[7 + n])
+            loads[f"new{row}"].start()
+
     def heads(n):
         def block(o):
             return zb.at[n, pl.ds(pl.multiple_of(o * CH, CH), CH)]
@@ -373,16 +412,24 @@
         base = Z0 + 8 * n
         low = [rem(z + NZ - s, NZ) for s in range(4)]
         high = [rem(z + s, NZ) for s in range(5)]
-        for s in (2, 1):
-            send(block(z), block(z), at_z(z + s), base + 2 * s - 2)
-            send(block(z), block(z), at_z(z - s), base + 2 * s - 1)
+        if n < CHUNKS - 1:
+            send(block(z), block(z), at_z(z + 2), base + 2)
+            send(block(z), block(z), at_z(z - 2), base + 3)
+        else:
+            first = [remote(block(z), block(z), at_z(z + 2 * w), base + 2 + (1 - w) // 2) for w in (1, -1)]
+            for copy in first:
+                copy.start()
+            for copy in first:
+                copy.wait_send()
+        send(block(z), block(z), at_z(z + 1), base)
+        send(block(z), block(z), at_z(z - 1), base + 1)
         yield
         arrived(block(low[2]), base + 2)
+        send(half(low[2], 0), half(low[2], 0), at_z(z + 2), base + 6)
         send(block(low[2]), block(low[2]), at_z(z + 1), base + 4)
-        send(half(low[2], 0), half(low[2], 0), at_z(z + 2), base + 6)
         arrived(block(high[2]), base + 3)
+        send(half(high[2], 1), half(high[2], 1), at_z(z - 2), base + 7)
         send(block(high[2]), block(high[2]), at_z(z - 1), base + 5)
-        send(half(high[2], 1), half(high[2], 1), at_z(z - 2), base + 7)
         yield
         arrived(block(low[1]), base)
         arrived(block(high[1]), base + 1)
@@ -397,38 +444,58 @@
             sx[n, i] = lax.dot_general(
                 zb[n], w_v[2 * (1 - c) + i], NT, preferred_element_type=jnp.float32
             ).astype(jnp.bfloat16)
-        send(sx.at[n], rx.at[n], partner, CX + n)
+            send(sx.at[n, i], rx.at[n, i], partner, CX + 2 * n + i)
         for i in range(2):
             own[n, i] = lax.dot_general(zb[n], w_v[2 * c + i], NT, preferred_element_type=jnp.float32)
 
     def sums(n):
         base = RS + 16 * n
-        arrived(rx.at[n], CX + n)
+
+        @pl.when(rem(x, 2) == 1)
+        def _():
+            rr[n, 4] = jnp.zeros((2, CH, COLS), jnp.bfloat16)
+
         for i in range(2):
+            arrived(rx.at[n, i], CX + 2 * n + i)
             ss[n, i] = (own[n, i] + rx[n, i].astype(jnp.float32)).astype(jnp.bfloat16)
         mine = rem(x, 2)
-        for s in (4, 3, 5, 2, 6, 1, 7, 0):
-            rows = pl.ds(pl.multiple_of(rem(y + s, NY) * CH, CH), CH)
-            for i in range(2):
-                copy = remote(
-                    ss.at[n, i, rows], rr.at[n, s, mine], owner(c, i, s), base + 2 * s + i, base + 2 * s + mine
-                )
-                if s == 0:
-                    pl.when(jnp.logical_not(itself(i)))(copy.start)
-
-                    @pl.when(itself(i))
-                    def _():
-                        rr[n, 0, mine] = ss[n, i, rows, :]
-                else:
-                    copy.start()
-                    sent.append(copy)
+
+        def rows_of(s):
+            return pl.ds(pl.multiple_of(rem(y + s, NY) * CH, CH), CH)
+
+        def deliver(s, i):
+            return remote(
+                ss.at[n, i, rows_of(s)], rr.at[n, s, mine], owner(c, i, s), base + 2 * s + i, base + 2 * s + mine
+            )
+
+        send(ss.at[n, 1, rows_of(4)], relay.at[n], at_y(y - 2), RL + n)
+        for s, i in ((4, 0), (3, 0), (3, 1), (5, 0), (5, 1), (2, 0), (2, 1), (6, 0), (1, 0), (1, 1), (7, 0), (7, 1)):
+            copy = deliver(s, i)
+            copy.start()
+            sent.append(copy)
+        for i in range(2):
+            pl.when(jnp.logical_not(itself(i)))(deliver(0, i).start)
+
+            @pl.when(itself(i))
+            def _():
+                rr[n, 0, mine] = ss[n, i, rows_of(0), :]
+        yield
+        arrived(relay.at[n], RL + n)
+        ss[n, 1, rows_of(6)] = (
+            ss[n, 1, rows_of(6), :].astype(jnp.float32) + relay[n].astype(jnp.float32)
+        ).astype(jnp.bfloat16)
+        copy = deliver(6, 1)
+        copy.start()
+        sent.append(copy)
         yield
         for e in range(2):
             total = None
-            for s in (0, 1, 7, 2, 6, 3, 5, 4):
+            for s in (0, 1, 7, 2, 3, 5, 4, 6):
                 copy = remote(rr.at[n, s, e], rr.at[n, s, e], partner, base + 2 * s + e)
                 if s == 0:
                     pl.when(jnp.logical_not(itself(e)))(copy.wait_recv)
+                elif s == 4:
+                    pl.when(mine == 0)(copy.wait_recv)
                 else:
                     copy.wait_recv()
                 part = rr[n, s, e].astype(jnp.float32)
@@ -476,90 +543,26 @@
             )
             out_ref[rows, :] = (res_v[rows, :].astype(jnp.float32) + placed).astype(jnp.bfloat16)
 
-    w = weights()
-    p = pages_out()
-    r = pages_ring()
-    hs = [heads(n) for n in range(CHUNKS)]
-    rs = [sums(n) for n in range(CHUNKS)]
-
-    next(p)
-    next(w)
-    order_send()
-    loads["q"].wait()
-    loads["kt"].wait()
-    prefix_part(0)
-    loads["vup"].wait()
-    own_part(0)
-    next(hs[0])
-    next(p, None)
-    next(r)
-    prefix_part(1)
-    own_part(1)
-    next(hs[1])
-    next(r)
-    next(r)
-    next(hs[0])
-    next(w)
-    next(r)
-    next(r)
-    prefix_part(2)
-    next(hs[1])
-    next(r)
-    next(r)
-    next(w)
-    next(r)
-    own_part(2)
-    next(hs[2])
-    next(hs[0])
-    product(0)
-    next(rs[0])
-    next(hs[2])
-    next(hs[1])
-    product(1)
-    next(rs[1])
-    next(rs[0])
-    order_wait()
-    next(hs[2])
-    product(2)
-    next(rs[1])
-    next(rs[2])
-    next(rs[2])
+    running = {"p": pages_out(), "w": weights(), "r": pages_ring()}
+    for n in range(CHUNKS):
+        running[f"h{n}"] = heads(n)
+        running[f"s{n}"] = sums(n)
+    for step in PLAN:
+        if step in running:
+            next(running[step])
+        elif step == "o":
+            order_send()
+        elif step == "O":
+            order_wait()
+        elif step == "n":
+            new_pool()
+        else:
+            {"a": prefix_part, "b": own_part, "m": product}[step[0]](int(step[1]))
     finish()
     for copy in sent:
         copy.wait_send()
-    loads["come"].wait()
-
-
-PARTS = 4
-
-
-def place_pages(page_s, move_s, pool_h, come_h, new_h, pool_v, come_v, sem):
-    size = POOL // PARTS
-    come = pltpu.make_async_copy(come_h, come_v, sem.at[2 * PARTS])
-    come.start()
-    parts = [pl.ds(n * size, size) for n in range(PARTS)]
-    loads = [pltpu.make_async_copy(pool_h.at[part], pool_v.at[part], sem.at[n]) for n, part in enumerate(parts)]
-    stores = [pltpu.make_async_copy(pool_v.at[part], new_h.at[part], sem.at[PARTS + n]) for n, part in enumerate(parts)]
-    for load in loads:
-        load.start()
-    come.wait()
-    for n in range(PARTS):
-        loads[n].wait()
-
-        def place(k, _):
-            slot = move_s[0, 0, k]
-            for p in range(2):
-                page = page_s[p, slot]
-
-                @pl.when((page >= n * size) & (page < (n + 1) * size))
-                def _():
-                    pool_v[page] = come_v[2 * k + p]
-            return 0
-
-        lax.fori_loop(0, MOVES, place, 0)
-        stores[n].start()
-    for store in stores:
-        store.wait()
+    loads["new0"].wait()
+    loads["new1"].wait()
 
 
 def local(
@@ -573,27 +576,27 @@
     hbm = pl.BlockSpec(memory_space=pl.ANY)
     bf, f32 = jnp.bfloat16, jnp.float32
     vm = pltpu.VMEM
-    layer_out, come = pl.pallas_call(
+    layer_out, new_pool = pl.pallas_call(
         fused,
         out_shape=(
             jax.ShapeDtypeStruct((2 * REQ, COLS), bf),
-            jax.ShapeDtypeStruct((CH * 2 * PAGE, LAT), bf),
+            jax.ShapeDtypeStruct((POOL, PAGE, LAT), bf),
         ),
         in_specs=[smem] * 4 + [vmem] * 2 + [hbm] * 6,
         out_specs=(vmem, hbm),
         scratch_shapes=[
-            vm((REQ, HEADS, LAT), bf), vm((POOL, PAGE, LAT), bf), vm((2, LAT, PLEN), bf),
+            vm((REQ, HEADS, LAT), bf), vm((POOL + 2 * MOVES, PAGE, LAT), bf), vm((2, LAT, PLEN), bf),
             vm((HEADS, KVL, VH), bf), vm((NX, COLS, DEPTH), bf), vm((2 * REQ, COLS), bf),
             vm((REQ, 128), bf), vm((2, REQ, 128), bf),
-            vm((8, 128), jnp.int32), pltpu.SMEM((8, 128), jnp.int32),
+            vm((16, 128), jnp.int32), pltpu.SMEM((16, 128), jnp.int32),
             vm((8, PAGE, LAT), bf), vm((128, PAGE, LAT), bf), vm((CH, HEADS, LAT), f32),
-            vm((CH * 2 * PAGE, LAT), bf), vm((3, CH, HEADS, 128), jnp.int32), vm((ROWS, KVL), f32),
+            vm((2 * CH, PAGE, LAT), bf), vm((3, CH, HEADS, 128), jnp.int32), vm((ROWS, KVL), f32),
             vm((2, ROWS, 128), f32), vm((KVL // 128, ROWS, 128), f32),
             vm((CHUNKS, NZ * CH, DEPTH), bf), vm((CHUNKS, 2, NZ * CH, COLS), bf),
             vm((CHUNKS, 2, NZ * CH, COLS), bf), vm((CHUNKS, 2, NZ * CH, COLS), f32),
             vm((CHUNKS, 2, NZ * CH, COLS), bf), vm((CHUNKS, NY, 2, CH, COLS), bf),
-            vm((2, REQ, COLS), f32),
-            pltpu.SemaphoreType.DMA((8,)),
+            vm((CHUNKS, CH, COLS), bf), vm((2, REQ, COLS), f32), vm((POOL, PAGE, LAT), bf),
+            pltpu.SemaphoreType.DMA((9,)),
             pltpu.SemaphoreType.DMA((SEMS,)),
             pltpu.SemaphoreType.DMA((SEMS,)),
         ],
@@ -605,17 +608,6 @@
         pages, prefix_id, lengths, prefix_len, pages, moves,
         queries, page_pool, prefix_cache.transpose(0, 2, 1), value_up, output_weight.T, residual,
     )
-    new_pool = pl.pallas_call(
-        place_pages,
-        out_shape=jax.ShapeDtypeStruct((POOL, PAGE, LAT), bf),
-        in_specs=[smem] * 2 + [hbm] * 2,
-        out_specs=hbm,
-        scratch_shapes=[
-            vm((POOL, PAGE, LAT), bf), vm((2 * MOVES, PAGE, LAT), bf), pltpu.SemaphoreType.DMA((2 * PARTS + 1,))
-        ],
-        compiler_params=pltpu.CompilerParams(vmem_limit_bytes=60 * 1024 * 1024),
-        name="place_pages",
-    )(pages, moves, page_pool, come.reshape(2 * MOVES, PAGE, LAT))
     return (layer_out, new_pool)
 
 

time: 81.5 us -> 77 us (0.945)
  Pallas kernels: 80 us -> 70.2 us
  local copies, waits for them, and re-layouts: 0.65 us -> 5.91 us
    pallas_call x1 -> x0, Pallas kernels: 6.95 us -> none  [local(): pl.pallas_call(place_pages, out_shape=jax.ShapeDtypeStruct((POOL, PAGE, L...]
    unnamed x3 -> x2, local copies, waits for them, and re-layouts: 0.65 us -> 5.91 us
    pallas_call x1, Pallas kernels: 73.1 us -> 70.2 us  [local(): pl.pallas_call(fused, out_shape=(jax.ShapeDtypeStruct((2 * REQ, COLS), bf...]
where the time goes in v3:
time: 77 us; the launch traced here: 76.8 us
  Pallas kernels  70.2 us (91%)
  local copies, waits for them, and re-layouts  5.91 us (8%)
    pallas_call x1, Pallas kernels, local(): pl.pallas_call(fused, out_shape=(jax.ShapeDtypeStruct((2 * REQ, COLS), bf...  70.2 us
    unnamed x2, local copies, waits for them, and re-layouts  5.91 us

profile of v3, /device:TPU:1, one launch (start us, length us, event | category | flops | bytes accessed | tf_op | source)
XLA Modules:
  0.0 76.8 jit_solution(5821919087350833389)
XLA Ops:
  0.6 70.2 %attention_block.1 = (bf16[192,224]{1,0:T(8,128)(2,1)}, bf16[192,16,576]{2,1,0:T(8,128)(2,1)}) custom-call(s32[2,96]{1,0:T(2,128)} %bitcast.6, s32[96]{0:T(128)} %prefix_s.1, s32[96]{0:T(128)} %length_s.1, s32[2]{0:T(128)} %limit_s.1, s32[2,96]{1,0:T(2,128)} %bitcast.7, s32[3,1,32]{2,1,0:T(1,128)} %bitcast.8, bf16[96,8,576]{2,1,0:T(8,128)(2,1)} %q_h.1, ...), custom_call_target="tpu_custom_call" | custom-call | tf_op jit(solution)/shard_map/attention_block/pallas_call | solution.py:579
  70.9 1.5 %copy.15 = bf16[192,224]{1,0:T(8,128)(2,1)} copy(bf16[192,224]{1,0:T(8,128)(2,1)} %get-tuple-element.4) | data formatting | bytes 172032
  72.4 4.4 %copy.16 = bf16[192,16,576]{2,1,0:T(8,128)(2,1)} copy(bf16[192,16,576]{2,1,0:T(8,128)(2,1)} %get-tuple-element.5) | data formatting | bytes 7077888

commit v4 on v3

--- a/solution.py
+++ b/solution.py
@@ -565,6 +565,28 @@
     loads["new1"].wait()
 
 
+PARTS = 4
+
+
+def settle(pool_h, layer_h, pool_o, layer_o, pool_v, layer_v, sem):
+    parts = [pl.ds(n * (POOL // PARTS), POOL // PARTS) for n in range(PARTS)]
+    loads = [pltpu.make_async_copy(pool_h.at[part], pool_v.at[part], sem.at[n]) for n, part in enumerate(parts)]
+    stores = [pltpu.make_async_copy(pool_v.at[part], pool_o.at[part], sem.at[PARTS + n]) for n, part in enumerate(parts)]
+    load = pltpu.make_async_copy(layer_h, layer_v, sem.at[2 * PARTS])
+    store = pltpu.make_async_copy(layer_v, layer_o, sem.at[2 * PARTS + 1])
+    for copy in loads:
+        copy.start()
+    load.start()
+    for n in range(PARTS):
+        loads[n].wait()
+        stores[n].start()
+    load.wait()
+    store.start()
+    for copy in stores:
+        copy.wait()
+    store.wait()
+
+
 def local(
     queries, page_pool, prefix_cache, page_table, lengths, prefix_id, prefix_len,
     move_list, value_up, output_weight, residual,
@@ -608,6 +630,17 @@
         pages, prefix_id, lengths, prefix_len, pages, moves,
         queries, page_pool, prefix_cache.transpose(0, 2, 1), value_up, output_weight.T, residual,
     )
+    new_pool, layer_out = pl.pallas_call(
+        settle,
+        out_shape=(jax.ShapeDtypeStruct(new_pool.shape, bf), jax.ShapeDtypeStruct(layer_out.shape, bf)),
+        in_specs=[hbm] * 2,
+        out_specs=(hbm, hbm),
+        scratch_shapes=[
+            vm(new_pool.shape, bf), vm(layer_out.shape, bf), pltpu.SemaphoreType.DMA((2 * PARTS + 2,))
+        ],
+        compiler_params=pltpu.CompilerParams(vmem_limit_bytes=60 * 1024 * 1024),
+        name="settle",
+    )(new_pool, layer_out)
     return (layer_out, new_pool)
 
 

time: 77 us -> 74.2 us (0.964)
  local copies, waits for them, and re-layouts: 5.91 us -> 0 us
  Pallas kernels: 70.2 us -> 73.4 us
    unnamed x2 -> x0, local copies, waits for them, and re-layouts: 5.91 us -> none
    pallas_call x0 -> x1, Pallas kernels: none -> 3.22 us  [local(): pl.pallas_call(settle, out_shape=(jax.ShapeDtypeStruct(new_pool.shape, bf...]
where the time goes in v4:
time: 74.2 us; the launch traced here: 74.1 us
  Pallas kernels  73.4 us (99%)
    pallas_call x1, Pallas kernels, local(): pl.pallas_call(fused, out_shape=(jax.ShapeDtypeStruct((2 * REQ, COLS), bf...  70.2 us
    pallas_call x1, Pallas kernels, local(): pl.pallas_call(settle, out_shape=(jax.ShapeDtypeStruct(new_pool.shape, bf...  3.22 us

profile of v4, /device:TPU:1, one launch (start us, length us, event | category | flops | bytes accessed | tf_op | source)
XLA Modules:
  0.0 74.1 jit_solution(7231912139750170504)
XLA Ops:
  0.6 70.2 %attention_block.1 = (bf16[192,224]{1,0:T(8,128)(2,1)}, bf16[192,16,576]{2,1,0:T(8,128)(2,1)}) custom-call(s32[2,96]{1,0:T(2,128)} %bitcast.6, s32[96]{0:T(128)} %prefix_s.1, s32[96]{0:T(128)} %length_s.1, s32[2]{0:T(128)} %limit_s.1, s32[2,96]{1,0:T(2,128)} %bitcast.7, s32[3,1,32]{2,1,0:T(1,128)} %bitcast.8, bf16[96,8,576]{2,1,0:T(8,128)(2,1)} %q_h.1, ...), custom_call_target="tpu_custom_call" | custom-call | tf_op jit(solution)/shard_map/attention_block/pallas_call | solution.py:601
  70.9 3.2 %settle.1 = (bf16[192,16,576]{2,1,0:T(8,128)(2,1)}, bf16[192,224]{1,0:T(8,128)(2,1)}) custom-call(bf16[192,16,576]{2,1,0:T(8,128)(2,1)} %get-tuple-element.6.pool_h, bf16[192,224]{1,0:T(8,128)(2,1)} %get-tuple-element.7.layer_h), custom_call_target="tpu_custom_call" | custom-call | tf_op jit(solution)/shard_map/settle/pallas_call | solution.py:633

commit v5 on v4

--- a/solution.py
+++ b/solution.py
@@ -29,8 +29,8 @@
 
 PLAN = (
     "p", "w", "a0", "b0", "h0", "r", "a1", "b1", "h1", "o", "r", "h0", "w", "r", "a2", "h1", "r", "w",
-    "h0", "m0", "r", "b2", "h2", "s0", "h1", "m1", "h2", "s1", "s0", "n", "s1", "O", "h2", "m2", "s2",
-    "s0", "s2", "s1", "s2",
+    "h0", "m0", "r", "b2", "h2", "s0", "h1", "m1", "h2", "s1", "s0", "n", "s1", "O", "h2", "m2", "k", "s2",
+    "d", "s0", "s2", "s1", "s2",
 )
 
 NT = (((1,), (1,)), ((), ()))
@@ -556,6 +556,12 @@
             order_wait()
         elif step == "n":
             new_pool()
+        elif step == "k":
+            older = sent[:]
+            del sent[:]
+        elif step == "d":
+            for copy in older:
+                copy.wait_send()
         else:
             {"a": prefix_part, "b": own_part, "m": product}[step[0]](int(step[1]))
     finish()

time: 74.2 us -> 74.1 us (level)
  no operation moved by 1% of the time
where the time goes in v5:
time: 74.1 us; the launch traced here: 73.9 us
  Pallas kernels  73.3 us (99%)
    pallas_call x1, Pallas kernels, local(): pl.pallas_call(fused, out_shape=(jax.ShapeDtypeStruct((2 * REQ, COLS), bf...  70.1 us
    pallas_call x1, Pallas kernels, local(): pl.pallas_call(settle, out_shape=(jax.ShapeDtypeStruct(new_pool.shape, bf...  3.22 us

profile of v5, /device:TPU:1, one launch (start us, length us, event | category | flops | bytes accessed | tf_op | source)
XLA Modules:
  0.0 73.9 jit_solution(2195897290331974370)
XLA Ops:
  0.6 70.1 %attention_block.1 = (bf16[192,224]{1,0:T(8,128)(2,1)}, bf16[192,16,576]{2,1,0:T(8,128)(2,1)}) custom-call(s32[2,96]{1,0:T(2,128)} %bitcast.6, s32[96]{0:T(128)} %prefix_s.1, s32[96]{0:T(128)} %length_s.1, s32[2]{0:T(128)} %limit_s.1, s32[2,96]{1,0:T(2,128)} %bitcast.7, s32[3,1,32]{2,1,0:T(1,128)} %bitcast.8, bf16[96,8,576]{2,1,0:T(8,128)(2,1)} %q_h.1, ...), custom_call_target="tpu_custom_call" | custom-call | tf_op jit(solution)/shard_map/attention_block/pallas_call | solution.py:607
  70.7 3.2 %settle.1 = (bf16[192,16,576]{2,1,0:T(8,128)(2,1)}, bf16[192,224]{1,0:T(8,128)(2,1)}) custom-call(bf16[192,16,576]{2,1,0:T(8,128)(2,1)} %get-tuple-element.6.pool_h, bf16[192,224]{1,0:T(8,128)(2,1)} %get-tuple-element.7.layer_h), custom_call_target="tpu_custom_call" | custom-call | tf_op jit(solution)/shard_map/settle/pallas_call | solution.py:639

commit v6 on v4

--- a/solution.py
+++ b/solution.py
@@ -38,7 +38,7 @@
 W0 = 0
 PD = W0 + 4
 PY = PD + 8
-PC = PY + 28
+PC = PY + 56
 Z0 = PC + 8
 CX = Z0 + 8 * CHUNKS
 RS = CX + 2 * CHUNKS
@@ -261,7 +261,7 @@
             come()
 
     def pages_ring():
-        parts = 4
+        parts = 8
 
         def part(o, k, core=c):
             return arr.at[pl.ds((o * 2 + core) * 8 + (8 // parts) * k, 8 // parts)]

time: 74.2 us -> 75.3 us (1.015)
  Pallas kernels: 73.4 us -> 74.2 us
    pallas_call x1, Pallas kernels: 70.2 us -> 71 us  [local(): pl.pallas_call(fused, out_shape=(jax.ShapeDtypeStruct((2 * REQ, COLS), bf...]
where the time goes in v6:
time: 75.3 us; the launch traced here: 74.9 us
  Pallas kernels  74.2 us (99%)
    pallas_call x1, Pallas kernels, local(): pl.pallas_call(fused, out_shape=(jax.ShapeDtypeStruct((2 * REQ, COLS), bf...  71 us
    pallas_call x1, Pallas kernels, local(): pl.pallas_call(settle, out_shape=(jax.ShapeDtypeStruct(new_pool.shape, bf...  3.22 us

profile of v6, /device:TPU:1, one launch (start us, length us, event | category | flops | bytes accessed | tf_op | source)
XLA Modules:
  0.0 74.9 jit_solution(9341526741373637105)
XLA Ops:
  0.6 71.0 %attention_block.1 = (bf16[192,224]{1,0:T(8,128)(2,1)}, bf16[192,16,576]{2,1,0:T(8,128)(2,1)}) custom-call(s32[2,96]{1,0:T(2,128)} %bitcast.6, s32[96]{0:T(128)} %prefix_s.1, s32[96]{0:T(128)} %length_s.1, s32[2]{0:T(128)} %limit_s.1, s32[2,96]{1,0:T(2,128)} %bitcast.7, s32[3,1,32]{2,1,0:T(1,128)} %bitcast.8, bf16[96,8,576]{2,1,0:T(8,128)(2,1)} %q_h.1, ...), custom_call_target="tpu_custom_call" | custom-call | tf_op jit(solution)/shard_map/attention_block/pallas_call | solution.py:601
  71.7 3.2 %settle.1 = (bf16[192,16,576]{2,1,0:T(8,128)(2,1)}, bf16[192,224]{1,0:T(8,128)(2,1)}) custom-call(bf16[192,16,576]{2,1,0:T(8,128)(2,1)} %get-tuple-element.6.pool_h, bf16[192,224]{1,0:T(8,128)(2,1)} %get-tuple-element.7.layer_h), custom_call_target="tpu_custom_call" | custom-call | tf_op jit(solution)/shard_map/settle/pallas_call | solution.py:633
